TPU v7x, 256 devices: a whole 4x4x8 slice. The times are simulated.
256 devices in a mesh: dp: 16 (over x, z_hi), tensor: 16 (over y, z_lo, core).
Axes of the slice: x: 4, y: 4, z: 8 (z_hi: 4, z_lo: 2; z = z_hi * 2 + z_lo), core: 2. Of those that a mesh axis runs over, the one named last changes fastest.
Arguments:
- hidden_in: bfloat16 [128, 16384], P('dp'), may hold values from -6 to 6
- norm_gain: float32 [16384], replicated, may hold values from 0.1 to 1.9
- w_query: bfloat16 [16384, 16384], P('dp', 'tensor'), may hold values from -0.046875 to 0.046875
- w_keyval: bfloat16 [16384, 2048], P('dp', 'tensor'), may hold values from -0.046875 to 0.046875
- w_out: bfloat16 [16384, 16384], P('tensor', 'dp'), may hold values from -0.046875 to 0.046875
- key_cache: bfloat16 [128, 16, 2048, 128], P('dp', 'tensor'), may hold values from -320 to 320
- value_cache: bfloat16 [128, 16, 2048, 128], P('dp', 'tensor'), may hold values from -6 to 6
- parent: int32 [128], P('dp'), may hold values from 0 to 127, as said below
- lengths: int32 [128], P('dp'), may hold values from 1 to 4096, as said below
Outputs:
- attended: bfloat16 [128, 16384], P('dp')
Inputs may be any that keep to these rules, and one draw needn't show every extreme that they name: parent[r] // 8 == r // 8: a row continues a cache of its own index of dp. `lengths`: every row has at least one cached position, and some row has all 4096.
All inputs are finite; a program needn't handle non-finite values.
Results may differ from a plain program's by a relative error of at most 0.012.
The roundings to bfloat16 on the way count: a program that leaves them out, or rounds other values in their place, can miss the bound.
Values may be sent and summed in bfloat16 or wider, within the bound.
No kernel may reach another device: no remote copies, remote signals or barrier semaphores. Data moves between devices by JAX's collectives and lax.ppermute only.
A program may use at most 64 MiB of HBM per device.

v0:
```python
import jax
import jax.numpy as jnp
from jax import lax
from jax.sharding import PartitionSpec as P


def swapped(value, axis, bit):
    mask = 2**bit
    pairs = [(source, source ^ mask) for source in range(lax.axis_size(axis))]
    return lax.ppermute(value, axis, pairs)


def rotate(t, pos):
    half = t.shape[-1] // 2
    inv = jnp.power(jnp.float32(500000.0), -jnp.arange(half, dtype=jnp.float32) * 2.0 / t.shape[-1])
    angle = pos[..., None] * inv
    cosine = jnp.cos(angle)
    sine = jnp.sin(angle)
    first = t[..., :half]
    second = t[..., half:]
    return jnp.concatenate(
        [first * cosine - second * sine, second * cosine + first * sine], axis=-1
    )


def per_device(
    hidden_in, norm_gain, w_query, w_keyval, w_out, key_cache, value_cache, parent, lengths
):
    rows_dev = hidden_in.shape[0]
    head_dim = key_cache.shape[3]
    half = key_cache.shape[2]
    cols_q = w_query.shape[1]
    heads_dev = cols_q // head_dim
    scale = head_dim ** (-0.5)
    xf = hidden_in.astype(jnp.float32)
    meansq = jnp.mean(xf * xf, axis=-1, keepdims=True)
    normed = (xf * lax.rsqrt(meansq + 1e-05) * norm_gain).astype(jnp.bfloat16)
    spread = lax.all_to_all(normed, "dp", split_axis=1, concat_axis=0, tiled=True)
    first = jnp.dot(spread, w_query, preferred_element_type=jnp.float32)
    second = jnp.dot(spread, w_keyval, preferred_element_type=jnp.float32)
    projected = lax.psum_scatter(
        jnp.concatenate([first, second], axis=1), "dp", scatter_dimension=0, tiled=True
    )
    pos = lengths.astype(jnp.float32)
    parity = lax.axis_index("tensor") % 2
    is_key = parity == 0
    queries_own = rotate(
        projected[:, :cols_q].reshape(rows_dev, heads_dev, head_dim), pos[:, None]
    ).astype(jnp.bfloat16)
    own_raw = projected[:, cols_q:]
    own_kv = jnp.where(is_key, rotate(own_raw, pos), own_raw).astype(jnp.bfloat16)
    queries_other, kv_other = swapped((queries_own, own_kv), "tensor", 0)
    queries = jnp.where(
        is_key,
        jnp.concatenate([queries_own, queries_other], axis=1),
        jnp.concatenate([queries_other, queries_own], axis=1),
    )
    new_key = jnp.where(is_key, own_kv, kv_other)
    new_value = jnp.where(is_key, kv_other, own_kv)
    local = parent - lax.axis_index("dp") * rows_dev
    keys = jnp.take(key_cache[:, 0], local, axis=0)
    values = jnp.take(value_cache[:, 0], local, axis=0)
    start_pos = parity * half
    position = start_pos + jnp.arange(half, dtype=jnp.int32)
    valid = position[None, :] < lengths[:, None]
    scores = jnp.einsum("rgd,rcd->rgc", queries, keys, preferred_element_type=jnp.float32) * scale
    scores = jnp.where(valid[:, None, :], scores, -jnp.inf)
    running = jnp.max(scores, axis=-1)
    safe = jnp.where(running == -jnp.inf, 0.0, running)
    weights = jnp.exp(scores - safe[..., None])
    summed = jnp.sum(weights, axis=-1)
    acc = jnp.einsum(
        "rgc,rcd->rgd", weights.astype(jnp.bfloat16), values, preferred_element_type=jnp.float32
    )
    newscore = (
        jnp.einsum("rgd,rd->rg", queries, new_key, preferred_element_type=jnp.float32) * scale
    )
    newscore = jnp.where(is_key, -jnp.inf, newscore)
    top = jnp.maximum(running, newscore)
    shrink = jnp.exp(running - top)
    newweight = jnp.exp(newscore - top)
    summed = summed * shrink + newweight
    acc = (
        acc * shrink[..., None]
        + newweight.astype(jnp.bfloat16).astype(jnp.float32)[..., None]
        * new_value.astype(jnp.float32)[:, None, :]
    )
    keep_acc = jnp.where(is_key, acc[:, :heads_dev], acc[:, heads_dev:])
    send_acc = jnp.where(is_key, acc[:, heads_dev:], acc[:, :heads_dev])
    keep_max = jnp.where(is_key, top[:, :heads_dev], top[:, heads_dev:])
    send_max = jnp.where(is_key, top[:, heads_dev:], top[:, :heads_dev])
    keep_sum = jnp.where(is_key, summed[:, :heads_dev], summed[:, heads_dev:])
    send_sum = jnp.where(is_key, summed[:, heads_dev:], summed[:, :heads_dev])
    other_acc, other_max, other_sum = swapped((send_acc, send_max, send_sum), "tensor", 0)
    highest = jnp.maximum(keep_max, other_max)
    mine_factor = jnp.exp(keep_max - highest)
    other_factor = jnp.exp(other_max - highest)
    total = keep_sum * mine_factor + other_sum * other_factor
    merged = (keep_acc * mine_factor[..., None] + other_acc * other_factor[..., None]) / total[
        ..., None
    ]
    heads = merged.reshape(rows_dev, heads_dev * head_dim).astype(jnp.bfloat16)
    partial_value = jnp.dot(
        lax.all_gather(heads, "dp", axis=0, tiled=True), w_out, preferred_element_type=jnp.float32
    )
    summed_all = lax.psum(partial_value, "tensor").astype(jnp.bfloat16)
    result = lax.all_to_all(summed_all, "dp", split_axis=0, concat_axis=1, tiled=True)
    return result


def solution(mesh):
    return jax.shard_map(
        per_device,
        mesh=mesh,
        in_specs=(
            P("dp", None),
            P(),
            P("dp", "tensor"),
            P("dp", "tensor"),
            P("tensor", "dp"),
            P("dp", "tensor", None, None),
            P("dp", "tensor", None, None),
            P("dp"),
            P("dp"),
        ),
        out_specs=P("dp", None),
        check_vma=False,
    )
```

profile of v0, /device:TPU:1, one launch (start us, length us, event | category | flops | bytes accessed | tf_op | source)
XLA Modules:
  0.0 328.3 jit_solution(14588569750835759376)
XLA Ops:
  6.5 1.3 fusion.19
  7.9 1.8 fusion.21
  9.7 11.6 %all-to-all-start = ((bf16[8,16,1024]{2,0,1:T(8,128)(2,1)}), bf16[8,16,1024]{2,0,1:T(8,128)(2,1)S(1)}, u32[]{:S(2)}, u32[]{:S(2)}) async-start(bf16[8,16,1024]{2,0,1:T(8,128)(2,1)} %bitcast), calls=%async_computation | async-start | bytes 524288 | tf_op jit(solution)/shard_map/all_to_all | solution.py:38
  21.3 0.7 convert_element_type.36
  22.0 0.7 compare_and_fusion
  22.8 10.9 %all-to-all-done = bf16[8,16,1024]{2,0,1:T(8,128)(2,1)S(1)} async-done(((bf16[8,16,1024]{2,0,1:T(8,128)(2,1)}), bf16[8,16,1024]{2,0,1:T(8,128)(2,1)S(1)}, u32[]{:S(2)}, u32[]{:S(2)}) %all-to-all-start) | async-done | bytes 262176 | tf_op jit(solution)/shard_map/all_to_all | solution.py:38
  34.4 0.9 pad_maximum_fusion
  35.3 5.2 %gather_fusion = bf16[8,2048,128]{2,1,0:T(8,128)(2,1)} fusion(bf16[8,2048,128]{2,1,0:T(8,128)(2,1)} %bitcast.32, s32[1024]{0:T(1024)S(1)} %pad_clamp_fusion), kind=kCustom, calls=%fused_computation.clone | custom fusion | bytes 8388640 | tf_op jit(solution)/shard_map/jit(_take)/gather | solution.py:61
  40.5 5.3 %gather_fusion.1 = bf16[8,2048,128]{2,1,0:T(8,128)(2,1)} fusion(bf16[8,2048,128]{2,1,0:T(8,128)(2,1)} %bitcast.33, s32[1024]{0:T(1024)S(1)} %pad_clamp_fusion), kind=kCustom, calls=%fused_computation.1.clone | custom fusion | bytes 8388640 | tf_op jit(solution)/shard_map/jit(_take)/gather | solution.py:62
  45.8 0.6 dynamic-slice
  47.1 142.3 %all-reduce.4.cloned.1.call-done = f32[128,1152]{1,0:T(8,128)} async-done(((f32[128,1152]{1,0:T(8,128)}), f32[128,1152]{1,0:T(8,128)}) %all-reduce.4.cloned.1.call-update) | async-done | bytes 589840
  189.4 0.9 multiply_subtract_fusion
  190.3 0.8 fusion.35
  191.1 11.1 %collective-permute-start.1 = (bf16[8,128]{1,0:T(8,128)(2,1)S(1)}, bf16[8,128]{1,0:T(8,128)(2,1)S(1)}, u32[]{:S(2)}, u32[]{:S(2)}) collective-permute-start(bf16[8,128]{1,0:T(8,128)(2,1)S(1)} %fusion.35), channel_id=1, source_target_pairs={{0,1},{1,0},{2,3},{3,2},{4,5},{5,4},{6,7},{7,6},{8,9},{9,8},{10,11... | collective-permute-start | bytes 6152 | tf_op jit(solution)/shard_map/ppermute | solution.py:10
  202.2 0.8 dynamic-slice_bitcast_fusion
  203.2 1.1 collective-permute-done
  204.6 3.7 %fusion.45 = (f32[8,16]{1,0:T(8,128)S(1)}, f32[8,16,2048]{2,1,0:T(8,128)S(1)}) fusion(bf16[8,2048,128]{2,1,0:T(8,128)(2,1)} %gather_fusion, pred[8]{0:T(512)(128)(4,1)S(1)} %get-tuple-element.13, bf16[8,8,128]{2,1,0:T(8,128)(2,1)S(1)} %collective-permute-done, bf16[8,8,64]{2,1,0:T(8,128)(2,1)S(1)} %get-tuple-element.18, ...), kind=kOutput, calls=%fused_computation.73 | convolution fusion | flops 70205312 | bytes 5292553 | tf_op jit(solution)/shard_map/rgd,rcd->rgc/dot_general | solution.py:66
  209.3 0.9 multiply_add_fusion
  210.6 1.0 collective-permute-done.3
  211.6 32.4 %all_gather.3 = bf16[128,1024]{1,0:T(8,128)(2,1)S(1)} all-gather(bf16[8,1024]{1,0:T(8,128)(2,1)S(1)} %bitcast.36), channel_id=1, replica_groups=mesh['dp'=16,'tensor'=16] {'dp'}, dimensions={0}, use_global_device_ids=true | all-gather | bytes 278528 | tf_op jit(solution)/shard_map/all_gather | solution.py:104
  244.0 0.4 fusion.46
  244.5 61.2 %all-reduce.5 = bf16[128,1024]{1,0:T(8,128)(2,1)S(1)} all-reduce(f32[128,1024]{1,0:T(8,128)S(1)} %fusion.46), channel_id=1, replica_groups=mesh['dp'=16,'tensor'=16] {'tensor'}, use_global_device_ids=true, to_apply=%region_4.6 | all-reduce | flops 131072 | bytes 786432 | tf_op jit(solution)/shard_map/psum | solution.py:106
  305.7 15.1 %all_to_all.38 = bf16[16,8,1024]{2,1,0:T(8,128)(2,1)S(1)} all-to-all(bf16[16,8,1024]{2,1,0:T(8,128)(2,1)S(1)} %bitcast.34), channel_id=1, replica_groups=mesh['dp'=16,'tensor'=16] {'dp'}, dimensions={0} | all-to-all | bytes 524288 | tf_op jit(solution)/shard_map/all_to_all | solution.py:107
  320.8 0.7 copy.34
  (43 shorter events, 2.9 us)
Async XLA Ops:
  6.5 27.1 %copy-start = (bf16[1024,1024]{1,0:T(8,128)(2,1)S(1)}, bf16[1024,1024]{1,0:T(8,128)(2,1)}, u32[]{:S(2)}) copy-start(bf16[1024,1024]{1,0:T(8,128)(2,1)} %param.13) | copy-start | bytes 6291460
  6.5 27.6 %copy-start.3 = (bf16[1024,128]{1,0:T(8,128)(2,1)S(1)}, bf16[1024,128]{1,0:T(8,128)(2,1)}, u32[]{:S(2)}) copy-start(bf16[1024,128]{1,0:T(8,128)(2,1)} %param.14) | copy-start | bytes 786436
  9.7 24.0 %all-to-all-start = ((bf16[8,16,1024]{2,0,1:T(8,128)(2,1)}), bf16[8,16,1024]{2,0,1:T(8,128)(2,1)S(1)}, u32[]{:S(2)}, u32[]{:S(2)}) async-start(bf16[8,16,1024]{2,0,1:T(8,128)(2,1)} %bitcast), calls=%async_computation | async-start | bytes 524288 | tf_op jit(solution)/shard_map/all_to_all | solution.py:38
  21.3 168.2 %all-reduce.4.cloned.1.call-start = ((), (), s32[]{:S(2)}) async-start(), calls=%async_computation.2 | async-start | bytes 1179648
  40.5 5.3 %copy-start.5 = (u32[256]{0:T(256)S(1)}, u32[256]{0:T(256)}, u32[]{:S(2)}) copy-start(u32[256]{0:T(256)} %constant.63) | copy-start | bytes 3076
  40.5 6.5 %copy-start.4 = (s32[8]{0:T(128)S(1)}, s32[8]{0:T(128)}, u32[]{:S(2)}) copy-start(s32[8]{0:T(128)} %param.19) | copy-start | bytes 100
  191.1 12.1 %collective-permute-start.1 = (bf16[8,128]{1,0:T(8,128)(2,1)S(1)}, bf16[8,128]{1,0:T(8,128)(2,1)S(1)}, u32[]{:S(2)}, u32[]{:S(2)}) collective-permute-start(bf16[8,128]{1,0:T(8,128)(2,1)S(1)} %fusion.35), channel_id=1, source_target_pairs={{0,1},{1,0},{2,3},{3,2},{4,5},{5,4},{6,7},{7,6},{8,9},{9,8},{10,11... | collective-permute-start | bytes 6152 | tf_op jit(solution)/shard_map/ppermute | solution.py:10
  203.1 1.2 collective-permute-start
  204.5 4.8 %copy-start.1 = (bf16[8,2048,128]{2,1,0:T(8,128)(2,1)S(1)}, bf16[8,2048,128]{2,1,0:T(8,128)(2,1)}, u32[]{:S(2)}) copy-start(bf16[8,2048,128]{2,1,0:T(8,128)(2,1)} %gather_fusion.1) | copy-start | bytes 12582916
  208.3 35.7 %copy-start.2 = (bf16[1024,1024]{1,0:T(8,128)(2,1)S(1)}, bf16[1024,1024]{1,0:T(8,128)(2,1)}, u32[]{:S(2)}) copy-start(bf16[1024,1024]{1,0:T(8,128)(2,1)} %param.15) | copy-start | bytes 6291460
  208.7 1.8 collective-permute-start.2
  209.0 1.5 collective-permute-start.4
  210.2 1.3 collective-permute-start.3
Sparse Core Ops, SparseCore 0:
  35.4 154.0 all-reduce.3
where the time goes:
time: 331 us; the launch traced here: 328 us
  waiting for transfers between devices  155 us (47%)
  blocking collectives  109 us (33%)
  starting transfers between devices  23.6 us (7%)
  between operations  14.2 us (4%)
  local copies, waits for them, and re-layouts  12.6 us (4%)
  other arithmetic  7.93 us (2%)
  matrix products  5.86 us (2%)
    unnamed x2, waiting for transfers between devices  142 us
    psum x1, blocking collectives, per_device(): summed_all = lax.psum(partial_value, 'tensor').astype(jnp.bfloat16)  61.2 us
    all_gather x1, blocking collectives, per_device(): lax.all_gather(heads, 'dp', axis=0, tiled=True)  32.4 us
    all_to_all x1, blocking collectives, per_device(): lax.all_to_all(summed_all, 'dp', split_axis=0, concat_axis=1, tiled=True)  15.1 us
    ppermute x5, starting transfers between devices, swapped(): return lax.ppermute(value, axis, pairs)  12 us
    all_to_all x1, starting transfers between devices, per_device(): lax.all_to_all(normed, 'dp', split_axis=1, concat_axis=0, tiled=True)  11.6 us
    all_to_all x1, waiting for transfers between devices, per_device(): lax.all_to_all(normed, 'dp', split_axis=1, concat_axis=0, tiled=True)  10.9 us
  transfers between devices with their start and end apart: 7, of which 4 were waited for; matrix products, arithmetic and copies ran while one was open for 4% of the time, Pallas kernels for 0%

commit v1 on v0

--- a/solution.py
+++ b/solution.py
@@ -2,6 +2,16 @@
 import jax.numpy as jnp
 from jax import lax
 from jax.sharding import PartitionSpec as P
+
+
+def row_groups(columns):
+    return [[j * columns + (j ^ p) for p in range(columns)] for j in range(columns)]
+
+
+def exchange(value, groups):
+    return lax.all_to_all(
+        value, ("dp", "tensor"), 0, 0, tiled=True, axis_index_groups=groups
+    )
 
 
 def swapped(value, axis, bit):
@@ -38,9 +48,16 @@
     spread = lax.all_to_all(normed, "dp", split_axis=1, concat_axis=0, tiled=True)
     first = jnp.dot(spread, w_query, preferred_element_type=jnp.float32)
     second = jnp.dot(spread, w_keyval, preferred_element_type=jnp.float32)
-    projected = lax.psum_scatter(
-        jnp.concatenate([first, second], axis=1), "dp", scatter_dimension=0, tiled=True
+    parts = lax.all_to_all(
+        jnp.concatenate([first, second], axis=1).reshape(
+            lax.axis_size("dp"), rows_dev, cols_q + second.shape[1]
+        ),
+        "dp",
+        0,
+        0,
+        tiled=True,
     )
+    projected = jnp.sum(parts, axis=0)
     pos = lengths.astype(jnp.float32)
     parity = lax.axis_index("tensor") % 2
     is_key = parity == 0
@@ -100,11 +117,30 @@
         ..., None
     ]
     heads = merged.reshape(rows_dev, heads_dev * head_dim).astype(jnp.bfloat16)
+    blocks = lax.axis_size("dp")
+    spread_heads = lax.all_to_all(
+        lax.optimization_barrier(jnp.broadcast_to(heads[None], (blocks,) + heads.shape)),
+        "dp",
+        0,
+        0,
+        tiled=True,
+    )
     partial_value = jnp.dot(
-        lax.all_gather(heads, "dp", axis=0, tiled=True), w_out, preferred_element_type=jnp.float32
+        spread_heads.reshape(blocks * rows_dev, heads.shape[1]),
+        w_out,
+        preferred_element_type=jnp.float32,
+    ).astype(jnp.bfloat16)
+    groups = row_groups(blocks)
+    gathered = exchange(partial_value.reshape(blocks, rows_dev, w_out.shape[1]), groups)
+    block = jnp.sum(gathered.astype(jnp.float32), axis=0).astype(jnp.bfloat16)
+    pairs = [
+        (j * blocks + t, (j ^ t) * blocks + t) for j in range(blocks) for t in range(blocks)
+    ]
+    block = lax.ppermute(block, ("dp", "tensor"), pairs)
+    whole = exchange(
+        lax.optimization_barrier(jnp.broadcast_to(block[None], (blocks,) + block.shape)), groups
     )
-    summed_all = lax.psum(partial_value, "tensor").astype(jnp.bfloat16)
-    result = lax.all_to_all(summed_all, "dp", split_axis=0, concat_axis=1, tiled=True)
+    result = jnp.transpose(whole, (1, 0, 2)).reshape(rows_dev, blocks * block.shape[1])
     return result
 
 

time: 331 us -> 115 us (0.35)
  waiting for transfers between devices: 155 us -> 25.9 us
  blocking collectives: 109 us -> 45.6 us
  between operations: 14.2 us -> 0.24 us
    unnamed x2 -> x0, waiting for transfers between devices: 142 us -> none
    psum x1 -> x0, blocking collectives: 61.2 us -> none  [per_device(): summed_all = lax.psum(partial_value, 'tensor').astype(jnp.bfloat16)]
    all_gather x1 -> x0, blocking collectives: 32.4 us -> none  [per_device(): lax.all_gather(heads, 'dp', axis=0, tiled=True)]
    all_to_all x1 -> x3, blocking collectives: 15.1 us -> 45.6 us  [the longest x2 30.4 us: exchange(): lax.all_to_all(value, ('dp', 'tensor'), 0, 0, tiled=True, axis_index_grou...]
    ppermute x5, starting transfers between devices: 12 us -> 3.42 us  [swapped(): return lax.ppermute(value, axis, pairs)]
    all_to_all x0 -> x1, waiting for transfers between devices: none -> 7.9 us  [per_device(): lax.all_to_all(jnp.concatenate([first, second], axis=1).reshape(lax.axis_...]
    all_to_all x0 -> x1, starting transfers between devices: none -> 3.58 us  [per_device(): lax.all_to_all(jnp.concatenate([first, second], axis=1).reshape(lax.axis_...]
    ppermute x0 -> x1, waiting for transfers between devices: none -> 3.46 us  [per_device(): block = lax.ppermute(block, ('dp', 'tensor'), pairs)]
  transfers between devices with their start and end apart: 7 -> 8, of which waited for: 4 -> 6; matrix products, arithmetic and copies ran while one was open for 4% -> 10% of each run, Pallas kernels for 0% -> 0%
where the time goes in v1:
time: 115 us
  blocking collectives  45.6 us (40%)
  waiting for transfers between devices  25.9 us (23%)
  starting transfers between devices  20.5 us (18%)
  local copies, waits for them, and re-layouts  11.2 us (10%)
  matrix products  5.86 us (5%)
  other arithmetic  5.35 us (5%)
    all_to_all x2, blocking collectives, exchange(): lax.all_to_all(value, ('dp', 'tensor'), 0, 0, tiled=True, axis_index_grou...  30.4 us
    all_to_all x1, blocking collectives, per_device(): lax.all_to_all(lax.optimization_barrier(jnp.broadcast_to(heads[None], (bl...  15.2 us
    all_to_all x1, waiting for transfers between devices, per_device(): lax.all_to_all(normed, 'dp', split_axis=1, concat_axis=0, tiled=True)  12.4 us
    all_to_all x1, starting transfers between devices, per_device(): lax.all_to_all(normed, 'dp', split_axis=1, concat_axis=0, tiled=True)  11.6 us
    all_to_all x1, waiting for transfers between devices, per_device(): lax.all_to_all(jnp.concatenate([first, second], axis=1).reshape(lax.axis_...  7.9 us
    gather x1, local copies, waits for them, and re-layouts, per_device(): values = jnp.take(value_cache[:, 0], local, axis=0)  5.24 us
    gather x1, local copies, waits for them, and re-layouts, per_device(): keys = jnp.take(key_cache[:, 0], local, axis=0)  5.22 us
    dot_general x1, matrix products, per_device(): jnp.einsum('rgd,rcd->rgc', queries, keys, preferred_element_type=jnp.floa...  3.7 us
  transfers between devices with their start and end apart: 8, of which 6 were waited for; matrix products, arithmetic and copies ran while one was open for 10% of the time, Pallas kernels for 0%

profile of v1, /device:TPU:1, one launch (start us, length us, event | category | flops | bytes accessed | tf_op | source)
XLA Modules:
  0.0 114.7 jit_solution(17323706543197776536)
XLA Ops:
  0.0 1.3 %fusion.20 = f32[8]{0:T(128)S(1)} fusion(bf16[8,16384]{1,0:T(8,128)(2,1)} %param.11), kind=kLoop, calls=%fused_computation.21 | loop fusion | flops 393208 | bytes 262176 | tf_op jit(solution)/shard_map/reduce_sum | solution.py:46
  1.4 1.8 %fusion.22 = bf16[8,16384]{1,0:T(8,128)(2,1)} fusion(bf16[8,16384]{1,0:T(8,128)(2,1)} %param.11, f32[16384]{0:T(1024)} %param.12, f32[8]{0:T(128)S(1)} %add_rsqrt_fusion), kind=kLoop, calls=%fused_computation.23 | loop fusion | flops 524288 | bytes 589856 | tf_op jit(solution)/shard_map/convert_element_type | solution.py:47
  3.2 11.6 %all-to-all-start = ((bf16[8,16,1024]{2,0,1:T(8,128)(2,1)}), bf16[8,16,1024]{2,0,1:T(8,128)(2,1)S(1)}, u32[]{:S(2)}, u32[]{:S(2)}) async-start(bf16[8,16,1024]{2,0,1:T(8,128)(2,1)} %bitcast), calls=%async_computation | async-start | bytes 524288 | tf_op jit(solution)/shard_map/all_to_all | solution.py:48
  14.8 12.4 %all-to-all-done = bf16[8,16,1024]{2,0,1:T(8,128)(2,1)S(1)} async-done(((bf16[8,16,1024]{2,0,1:T(8,128)(2,1)}), bf16[8,16,1024]{2,0,1:T(8,128)(2,1)S(1)}, u32[]{:S(2)}, u32[]{:S(2)}) %all-to-all-start) | async-done | bytes 262176 | tf_op jit(solution)/shard_map/all_to_all | solution.py:48
  27.2 0.4 fusion.28
  27.8 0.9 maximum_bitcast_fusion
  28.7 3.6 %all-to-all-start.1 = ((f32[16,8,1152]{2,1,0:T(8,128)}), f32[16,8,1152]{2,1,0:T(8,128)S(1)}, u32[]{:S(2)}, u32[]{:S(2)}) async-start(f32[16,8,1152]{2,1,0:T(8,128)} %maximum_bitcast_fusion), calls=%async_computation.1 | async-start | bytes 1179648 | tf_op jit(solution)/shard_map/all_to_all | solution.py:51
  32.4 5.2 %gather_fusion = bf16[8,2048,128]{2,1,0:T(8,128)(2,1)} fusion(bf16[8,2048,128]{2,1,0:T(8,128)(2,1)} %bitcast.37, s32[1024]{0:T(1024)S(1)} %pad_clamp_fusion), kind=kCustom, calls=%fused_computation.clone | custom fusion | bytes 8388640 | tf_op jit(solution)/shard_map/jit(_take)/gather | solution.py:78
  37.6 5.2 %gather_fusion.1 = bf16[8,2048,128]{2,1,0:T(8,128)(2,1)} fusion(bf16[8,2048,128]{2,1,0:T(8,128)(2,1)} %bitcast.38, s32[1024]{0:T(1024)S(1)} %pad_clamp_fusion), kind=kCustom, calls=%fused_computation.1.clone | custom fusion | bytes 8388640 | tf_op jit(solution)/shard_map/jit(_take)/gather | solution.py:79
  43.1 7.9 %all-to-all-done.1 = f32[16,8,1152]{2,1,0:T(8,128)S(1)} async-done(((f32[16,8,1152]{2,1,0:T(8,128)}), f32[16,8,1152]{2,1,0:T(8,128)S(1)}, u32[]{:S(2)}, u32[]{:S(2)}) %all-to-all-start.1) | async-done | bytes 589856 | tf_op jit(solution)/shard_map/all_to_all | solution.py:51
  51.2 2.5 %collective-permute-start.1 = (bf16[8,128]{1,0:T(8,128)(2,1)S(1)}, bf16[8,128]{1,0:T(8,128)(2,1)S(1)}, u32[]{:S(2)}, u32[]{:S(2)}) collective-permute-start(bf16[8,128]{1,0:T(8,128)(2,1)S(1)} %fusion.37), channel_id=1, source_target_pairs={{0,1},{1,0},{2,3},{3,2},{4,5},{5,4},{6,7},{7,6},{8,9},{9,8},{10,11... | collective-permute-start | bytes 6152 | tf_op jit(solution)/shard_map/ppermute | solution.py:20
  54.0 0.6 collective-permute-done.1
  54.6 0.6 collective-permute-done
  55.3 3.7 %fusion.46 = (f32[8,16]{1,0:T(8,128)S(1)}, f32[8,16,2048]{2,1,0:T(8,128)S(1)}) fusion(bf16[8,2048,128]{2,1,0:T(8,128)(2,1)} %gather_fusion, pred[8]{0:T(512)(128)(4,1)S(1)} %get-tuple-element.13, bf16[8,8,128]{2,1,0:T(8,128)(2,1)S(1)} %collective-permute-done, bf16[8,8,64]{2,1,0:T(8,128)(2,1)S(1)} %get-tuple-element.16, ...), kind=kOutput, calls=%fused_computation.75 | convolution fusion | flops 70205312 | bytes 5292553 | tf_op jit(solution)/shard_map/rgd,rcd->rgc/dot_general | solution.py:83
  59.8 0.3 collective-permute-start.4
  60.1 0.9 multiply_add_fusion
  61.3 1.0 collective-permute-done.3
  62.4 15.2 %all_to_all.39 = bf16[16,8,1024]{2,1,0:T(8,128)(2,1)S(1)} all-to-all(bf16[16,8,1024]{2,1,0:T(8,128)(2,1)S(1)} %broadcast_in_dim.34), channel_id=1, replica_groups=mesh['dp'=16,'tensor'=16] {'dp'}, dimensions={0} | all-to-all | bytes 524288 | tf_op jit(solution)/shard_map/all_to_all | solution.py:121
  77.7 0.5 fusion.14
  78.2 13.7 %all_to_all.40 = bf16[16,8,1024]{2,1,0:T(8,128)(2,1)S(1)} all-to-all(bf16[16,8,1024]{2,1,0:T(8,128)(2,1)S(1)} %fusion.14), channel_id=1, replica_groups={{0,1,2,3,4,5,6,7,8,9,10,11,12,13,14,15},{17,16,19,18,21,20,23,22,25,24,..., dimensions={0} | all-to-all | bytes 524288 | tf_op jit(solution)/shard_map/all_to_all | solution.py:12
  91.9 1.9 %collective-permute-start.5 = (bf16[8,1024]{1,0:T(8,128)(2,1)S(1)}, bf16[8,1024]{1,0:T(8,128)(2,1)S(1)}, u32[]{:S(2)}, u32[]{:S(2)}) collective-permute-start(bf16[8,1024]{1,0:T(8,128)(2,1)S(1)} %reduce_sum.42), channel_id=1, source_target_pairs={{0,0},{1,17},{2,34},{3,51},{4,68},{5,85},{6,102},{7,119},{8,136},{... | collective-permute-start | bytes 49160 | tf_op jit(solution)/shard_map/ppermute | solution.py:139
  93.8 3.5 %collective-permute-done.5 = bf16[8,1024]{1,0:T(8,128)(2,1)S(1)} collective-permute-done((bf16[8,1024]{1,0:T(8,128)(2,1)S(1)}, bf16[8,1024]{1,0:T(8,128)(2,1)S(1)}, u32[]{:S(2)}, u32[]{:S(2)}) %collective-permute-start.5) | collective-permute-done | bytes 16416 | tf_op jit(solution)/shard_map/ppermute | solution.py:139
  97.3 16.6 %all_to_all.41 = bf16[16,8,1024]{2,1,0:T(8,128)(2,1)S(1)} all-to-all(bf16[16,8,1024]{2,1,0:T(8,128)(2,1)S(1)} %broadcast_in_dim.35), channel_id=1, replica_groups={{0,1,2,3,4,5,6,7,8,9,10,11,12,13,14,15},{17,16,19,18,21,20,23,22,25,24,..., dimensions={0} | all-to-all | bytes 524288 | tf_op jit(solution)/shard_map/all_to_all | solution.py:12
  114.0 0.7 copy.23
  (47 shorter events, 2.4 us)
Async XLA Ops:
  0.0 27.2 %copy-start = (bf16[1024,1024]{1,0:T(8,128)(2,1)S(1)}, bf16[1024,1024]{1,0:T(8,128)(2,1)}, u32[]{:S(2)}) copy-start(bf16[1024,1024]{1,0:T(8,128)(2,1)} %param.13) | copy-start | bytes 6291460
  0.0 27.6 %copy-start.3 = (bf16[1024,128]{1,0:T(8,128)(2,1)S(1)}, bf16[1024,128]{1,0:T(8,128)(2,1)}, u32[]{:S(2)}) copy-start(bf16[1024,128]{1,0:T(8,128)(2,1)} %param.14) | copy-start | bytes 786436
  0.0 32.3 %copy-start.5 = (s32[8]{0:T(128)S(1)}, s32[8]{0:T(128)}, u32[]{:S(2)}) copy-start(s32[8]{0:T(128)} %param.18) | copy-start | bytes 100
  0.0 32.4 %copy-start.4 = (s32[8]{0:T(128)S(1)}, s32[8]{0:T(128)}, u32[]{:S(2)}) copy-start(s32[8]{0:T(128)} %param.19) | copy-start | bytes 100
  3.2 24.0 %all-to-all-start = ((bf16[8,16,1024]{2,0,1:T(8,128)(2,1)}), bf16[8,16,1024]{2,0,1:T(8,128)(2,1)S(1)}, u32[]{:S(2)}, u32[]{:S(2)}) async-start(bf16[8,16,1024]{2,0,1:T(8,128)(2,1)} %bitcast), calls=%async_computation | async-start | bytes 524288 | tf_op jit(solution)/shard_map/all_to_all | solution.py:48
  28.7 22.2 %all-to-all-start.1 = ((f32[16,8,1152]{2,1,0:T(8,128)}), f32[16,8,1152]{2,1,0:T(8,128)S(1)}, u32[]{:S(2)}, u32[]{:S(2)}) async-start(f32[16,8,1152]{2,1,0:T(8,128)} %maximum_bitcast_fusion), calls=%async_computation.1 | async-start | bytes 1179648 | tf_op jit(solution)/shard_map/all_to_all | solution.py:51
  51.2 3.3 %collective-permute-start.1 = (bf16[8,128]{1,0:T(8,128)(2,1)S(1)}, bf16[8,128]{1,0:T(8,128)(2,1)S(1)}, u32[]{:S(2)}, u32[]{:S(2)}) collective-permute-start(bf16[8,128]{1,0:T(8,128)(2,1)S(1)} %fusion.37), channel_id=1, source_target_pairs={{0,1},{1,0},{2,3},{3,2},{4,5},{5,4},{6,7},{7,6},{8,9},{9,8},{10,11... | collective-permute-start | bytes 6152 | tf_op jit(solution)/shard_map/ppermute | solution.py:20
  53.9 1.2 %collective-permute-start = (bf16[8,8,128]{2,1,0:T(8,128)(2,1)S(1)}, bf16[8,8,128]{2,1,0:T(8,128)(2,1)S(1)}, u32[]{:S(2)}, u32[]{:S(2)}) collective-permute-start(bf16[8,8,128]{2,1,0:T(8,128)(2,1)S(1)} %pad_maximum_fusion), channel_id=1, source_target_pairs={{0,1},{1,0},{2,3},{3,2},{4,5},{5,4},{6,7},{7,6},{8,9},{9,8},{10,11... | collective-permute-start | bytes 49160 | tf_op jit(solution)/shard_map/ppermute | solution.py:20
  55.3 4.8 %copy-start.1 = (bf16[8,2048,128]{2,1,0:T(8,128)(2,1)S(1)}, bf16[8,2048,128]{2,1,0:T(8,128)(2,1)}, u32[]{:S(2)}) copy-start(bf16[8,2048,128]{2,1,0:T(8,128)(2,1)} %gather_fusion.1) | copy-start | bytes 12582916
  59.4 18.3 %copy-start.2 = (bf16[1024,1024]{1,0:T(8,128)(2,1)S(1)}, bf16[1024,1024]{1,0:T(8,128)(2,1)}, u32[]{:S(2)}) copy-start(bf16[1024,1024]{1,0:T(8,128)(2,1)} %param.15) | copy-start | bytes 6291460
  59.5 1.8 %collective-permute-start.2 = (f32[8,8]{1,0:T(8,128)S(1)}, f32[8,8]{1,0:T(8,128)S(1)}, u32[]{:S(2)}, u32[]{:S(2)}) collective-permute-start(f32[8,8]{1,0:T(8,128)S(1)} %slice_select_fusion.3), channel_id=1, source_target_pairs={{0,1},{1,0},{2,3},{3,2},{4,5},{5,4},{6,7},{7,6},{8,9},{9,8},{10,11... | collective-permute-start | bytes 776 | tf_op jit(solution)/shard_map/ppermute | solution.py:20
  59.8 1.5 %collective-permute-start.4 = (f32[8,8]{1,0:T(8,128)S(1)}, f32[8,8]{1,0:T(8,128)S(1)}, u32[]{:S(2)}, u32[]{:S(2)}) collective-permute-start(f32[8,8]{1,0:T(8,128)S(1)} %slice_select_fusion.2), channel_id=1, source_target_pairs={{0,1},{1,0},{2,3},{3,2},{4,5},{5,4},{6,7},{7,6},{8,9},{9,8},{10,11... | collective-permute-start | bytes 776 | tf_op jit(solution)/shard_map/ppermute | solution.py:20
  61.0 1.3 %collective-permute-start.3 = (f32[8,8,128]{2,1,0:T(8,128)S(1)}, f32[8,8,128]{2,1,0:T(8,128)S(1)}, u32[]{:S(2)}, u32[]{:S(2)}) collective-permute-start(f32[8,8,128]{2,1,0:T(8,128)S(1)} %slice_select_fusion), channel_id=1, source_target_pairs={{0,1},{1,0},{2,3},{3,2},{4,5},{5,4},{6,7},{7,6},{8,9},{9,8},{10,11... | collective-permute-start | bytes 98312 | tf_op jit(solution)/shard_map/ppermute | solution.py:20
  91.9 5.4 %collective-permute-start.5 = (bf16[8,1024]{1,0:T(8,128)(2,1)S(1)}, bf16[8,1024]{1,0:T(8,128)(2,1)S(1)}, u32[]{:S(2)}, u32[]{:S(2)}) collective-permute-start(bf16[8,1024]{1,0:T(8,128)(2,1)S(1)} %reduce_sum.42), channel_id=1, source_target_pairs={{0,0},{1,17},{2,34},{3,51},{4,68},{5,85},{6,102},{7,119},{8,136},{... | collective-permute-start | bytes 49160 | tf_op jit(solution)/shard_map/ppermute | solution.py:139

commit v2 on v0

v2 whole, which is shorter than its diff:
```python
import jax
import jax.numpy as jnp
import numpy as np
from jax import lax
from jax.experimental import pallas as pl
from jax.experimental.pallas import tpu as pltpu
from jax.sharding import PartitionSpec as P

EPS = 1e-05
SCALE = 128.0
INVERSE = (500000.0 ** (-np.arange(64) * 2.0 / 128)).astype(np.float32)
VMEM = pl.BlockSpec(memory_space=pltpu.VMEM)
SMEM = pl.BlockSpec(memory_space=pltpu.SMEM)
HBM = pl.BlockSpec(memory_space=pltpu.HBM)


def index(x, z_hi, y, z_lo, core):
    return (x * 4 + z_hi) * 16 + y * 4 + z_lo * 2 + core


NEAR_GROUPS = [
    [index(x, z_hi, y, z_lo ^ (z_hi >> 1), core) for x in range(4) for z_hi in range(4)]
    for y in range(4)
    for z_lo in range(2)
    for core in range(2)
]


def holder(j, t):
    return t ^ 2 if t % 4 in (0, 2) else t


SUM_GROUPS = [[j * 16 + (j ^ p) for p in range(16)] for j in range(16)]
MOVES = [
    (j * 16 + t, (j ^ t) * 16 + holder(j, t)) for j in range(16) for t in range(16)
]
WHOLE_GROUPS = [[i * 16 + holder(p, i ^ p) for p in range(16)] for i in range(16)]


def exchange(value, groups):
    return lax.all_to_all(
        value, ("dp", "tensor"), 0, 0, tiled=True, axis_index_groups=groups
    )


def in_hbm(value):
    return pltpu.with_memory_space_constraint(value, pltpu.HBM)


def core_swap(value):
    return lax.ppermute(value, "tensor", [(t, t ^ 1) for t in range(16)])


def norm_kernel(
    hidden_hbm, gain_hbm, weight_hbm, lengths_hbm,
    out, weight, cosine_out, sine_out, kv_cosine_out, kv_sine_out,
    hidden, gain, lengths, sems,
):
    copies = [
        pltpu.make_async_copy(lengths_hbm, lengths, sems.at[0]),
        pltpu.make_async_copy(hidden_hbm, hidden, sems.at[1]),
        pltpu.make_async_copy(gain_hbm, gain, sems.at[2]),
        pltpu.make_async_copy(weight_hbm, weight, sems.at[3]),
    ]
    for copy in copies:
        copy.start()
    rows, hd = cosine_out.shape
    column = lax.broadcasted_iota(jnp.int32, (rows, hd), 1)
    row = lax.broadcasted_iota(jnp.int32, (rows, hd), 0)
    inv = jnp.zeros((rows, hd), jnp.float32)
    for k in range(hd // 2):
        inv = jnp.where(column % (hd // 2) == k, float(INVERSE[k]), inv)
    copies[0].wait()
    position = jnp.zeros((rows, hd), jnp.float32)
    for r in range(rows):
        position = jnp.where(row == r, lengths[r].astype(jnp.float32), position)
    angle = position * inv
    cosine = jnp.cos(angle)
    sine = jnp.where(column < hd // 2, -jnp.sin(angle), jnp.sin(angle))
    is_key = lax.axis_index("tensor") % 2 == 0
    cosine_out[...] = cosine
    sine_out[...] = sine
    kv_cosine_out[...] = jnp.where(is_key, cosine, 1.0)
    kv_sine_out[...] = jnp.where(is_key, sine, 0.0)
    copies[1].wait()
    xf = hidden[...].astype(jnp.float32)
    meansq = jnp.mean(xf * xf, axis=-1, keepdims=True)
    factor = lax.rsqrt(meansq + EPS)
    copies[2].wait()
    blocks, _, width = out.shape
    for k in range(blocks):
        part = slice(k * width, (k + 1) * width)
        out[k] = (xf[:, part] * factor * gain[:, part]).astype(jnp.bfloat16)
    copies[3].wait()


def rotate_kernel(total, cosine, sine, kv_cosine, kv_sine, out, turned):
    heads = total.shape[1] // 128 - 1
    for h in range(heads + 1):
        t = total[:, h * 128 : (h + 1) * 128]
        swapped = pltpu.roll(t, 64, 1)
        if h < heads:
            turned[:, h, :] = t * cosine[...] + swapped * sine[...]
        else:
            turned[:, h, :] = t * kv_cosine[...] + swapped * kv_sine[...]
    for r in range(8):
        out[r] = turned[r].astype(jnp.bfloat16)


def attention_kernel(
    parent, lengths, own, other, keys, value_cache, keep, send, values, weights, sems
):
    rows, _, half, hd = keys.shape
    base = lax.axis_index("dp") * rows
    parity = lax.axis_index("tensor") % 2
    copies = []
    for r in range(rows):
        src = parent[r] - base
        copies.append(
            pltpu.make_async_copy(value_cache.at[src, 0], values.at[r], sems.at[r])
        )
        copies[r].start()
    scale = hd ** (-0.5)
    second = parity == 1
    column = lax.broadcasted_iota(jnp.int32, (16, half), 1)
    found = []
    for r in range(rows):
        mine = own[r].astype(jnp.float32)
        theirs = other[r].astype(jnp.float32)
        queries = jnp.concatenate([mine[:8], theirs[:8]], axis=0)
        new_key = jnp.where(second, theirs[8:9], mine[8:9])
        new_value = jnp.where(second, mine[8:9], theirs[8:9])
        newscore = jnp.sum(queries * new_key, axis=-1, keepdims=True) * scale
        newscore = jnp.where(second, newscore, -jnp.inf)
        scores = lax.dot_general(
            queries.astype(jnp.bfloat16),
            keys[parent[r] - base, 0],
            (((1,), (1,)), ((), ())),
            preferred_element_type=jnp.float32,
        )
        limit = lengths[r] - parity * half
        scores = jnp.where(column < limit, scores * scale, -jnp.inf)
        top = jnp.maximum(jnp.max(scores, axis=-1, keepdims=True), newscore)
        weight = jnp.exp(scores - top)
        newweight = jnp.exp(newscore - top)
        total = jnp.sum(weight, axis=-1, keepdims=True) + newweight
        weights[r] = weight.astype(jnp.bfloat16)
        added = newweight.astype(jnp.bfloat16).astype(jnp.float32) * new_value
        found.append((added, top, total))
    for copy in copies:
        copy.wait()
    for r in range(rows):
        added, top, total = found[r]
        acc = jnp.dot(weights[r], values[r], preferred_element_type=jnp.float32) + added
        top = jnp.broadcast_to(top, acc.shape)
        total = jnp.broadcast_to(total, acc.shape)
        for k, part in enumerate((acc, top, total)):
            keep[:, r, k * hd : (k + 1) * hd] = part[:8]
            send[:, r, k * hd : (k + 1) * hd] = part[8:]


def merge_kernel(mine, theirs, out):
    hd = mine.shape[2] // 3
    for h in range(mine.shape[0]):
        a, b = mine[h], theirs[h]
        highest = jnp.maximum(a[:, hd : 2 * hd], b[:, hd : 2 * hd])
        fa = jnp.exp(a[:, hd : 2 * hd] - highest)
        fb = jnp.exp(b[:, hd : 2 * hd] - highest)
        total = a[:, 2 * hd :] * fa + b[:, 2 * hd :] * fb
        head = ((a[:, :hd] * fa + b[:, :hd] * fb) / total).astype(jnp.bfloat16)
        for k in range(out.shape[0]):
            out[k, :, h * hd : (h + 1) * hd] = head


def per_device(
    hidden_in, norm_gain, w_query, w_keyval, w_out, key_cache, value_cache, parent, lengths
):
    rows, d_model = hidden_in.shape
    hd = key_cache.shape[3]
    half = key_cache.shape[2]
    cols = w_query.shape[1]
    blocks = d_model // cols
    heads = cols // hd
    table = jax.ShapeDtypeStruct((rows, hd), jnp.float32)
    normed, w_keyval, *tables = pl.pallas_call(
        norm_kernel,
        out_shape=(
            jax.ShapeDtypeStruct((blocks, rows, cols), jnp.bfloat16),
            jax.ShapeDtypeStruct(w_keyval.shape, jnp.bfloat16),
        )
        + (table,) * 4,
        in_specs=[HBM] * 4,
        out_specs=(VMEM,) * 6,
        scratch_shapes=[
            pltpu.VMEM((rows, d_model), jnp.bfloat16),
            pltpu.VMEM((1, d_model), jnp.float32),
            pltpu.SMEM((rows,), jnp.int32),
            pltpu.SemaphoreType.DMA((4,)),
        ],
        compiler_params=pltpu.CompilerParams(vmem_limit_bytes=8 * 2**20),
    )(in_hbm(hidden_in), in_hbm(norm_gain[None]), in_hbm(w_keyval), in_hbm(lengths))
    spread = exchange(normed, NEAR_GROUPS).reshape(blocks * rows, cols)
    first = jnp.dot(spread, w_query, preferred_element_type=jnp.float32)
    second = jnp.dot(spread, w_keyval, preferred_element_type=jnp.float32)
    partial = jnp.concatenate([first, second], axis=1) * SCALE
    parts = lax.all_to_all(
        partial.astype(jnp.float16).reshape(blocks, rows, cols + hd), "dp", 0, 0, tiled=True
    ).astype(jnp.float32)
    own = pl.pallas_call(
        rotate_kernel,
        out_shape=jax.ShapeDtypeStruct((rows, 16, hd), jnp.bfloat16),
        in_specs=[VMEM] * 5,
        out_specs=VMEM,
        scratch_shapes=[pltpu.VMEM((rows, 16, hd), jnp.float32)],
        compiler_params=pltpu.CompilerParams(vmem_limit_bytes=8 * 2**20),
    )(jnp.sum(parts, axis=0) * (1.0 / SCALE), *tables)
    other = core_swap(own)
    shape = jax.ShapeDtypeStruct((heads, rows, 3 * hd), jnp.float32)
    keep, send = pl.pallas_call(
        attention_kernel,
        out_shape=(shape, shape),
        in_specs=[SMEM, SMEM, VMEM, VMEM, VMEM, HBM],
        out_specs=(VMEM, VMEM),
        scratch_shapes=[
            pltpu.VMEM((rows, half, hd), jnp.bfloat16),
            pltpu.VMEM((rows, 2 * heads, half), jnp.bfloat16),
            pltpu.SemaphoreType.DMA((rows,)),
        ],
        compiler_params=pltpu.CompilerParams(vmem_limit_bytes=24 * 2**20),
    )(parent, lengths, own, other, key_cache, in_hbm(value_cache))
    received = core_swap(send)
    copies = pl.pallas_call(
        merge_kernel,
        out_shape=jax.ShapeDtypeStruct((blocks, rows, cols), jnp.bfloat16),
        in_specs=[VMEM, VMEM],
        out_specs=VMEM,
        compiler_params=pltpu.CompilerParams(vmem_limit_bytes=8 * 2**20),
    )(keep, received)
    spread_heads = lax.all_to_all(copies, "dp", 0, 0, tiled=True)
    partial = jnp.dot(
        spread_heads.reshape(blocks * rows, cols), w_out, preferred_element_type=jnp.float32
    ).astype(jnp.bfloat16)
    gathered = exchange(partial.reshape(blocks, rows, cols), SUM_GROUPS)
    block = jnp.sum(gathered.astype(jnp.float32), axis=0).astype(jnp.bfloat16)
    block = lax.ppermute(block, ("dp", "tensor"), MOVES)
    block = lax.optimization_barrier(jnp.broadcast_to(block[None], (blocks, rows, cols)))
    whole = exchange(block, WHOLE_GROUPS)
    return jnp.transpose(whole, (1, 0, 2)).reshape(rows, d_model)


def solution(mesh):
    return jax.shard_map(
        per_device,
        mesh=mesh,
        in_specs=(
            P("dp", None),
            P(),
            P("dp", "tensor"),
            P("dp", "tensor"),
            P("tensor", "dp"),
            P("dp", "tensor", None, None),
            P("dp", "tensor", None, None),
            P("dp"),
            P("dp"),
        ),
        out_specs=P("dp", None),
        check_vma=False,
    )
```

time: 331 us -> 100 us (0.30)
  waiting for transfers between devices: 155 us -> 4.91 us
  blocking collectives: 109 us -> 83.6 us
  starting transfers between devices: 23.6 us -> 3.25 us
  between operations: 14.2 us -> 0.12 us
  local copies, waits for them, and re-layouts: 12.6 us -> 0.75 us
  other arithmetic: 7.93 us -> 0.15 us
  Pallas kernels: 0 us -> 6.05 us
  matrix products: 5.86 us -> 1.12 us
    unnamed x2 -> x0, waiting for transfers between devices: 142 us -> none
    all_to_all x1 -> x5, blocking collectives: 15.1 us -> 83.6 us  [the longest x3 52.4 us: exchange(): lax.all_to_all(value, ('dp', 'tensor'), 0, 0, tiled=True, axis_index_grou...]
    psum x1 -> x0, blocking collectives: 61.2 us -> none  [per_device(): summed_all = lax.psum(partial_value, 'tensor').astype(jnp.bfloat16)]
    all_gather x1 -> x0, blocking collectives: 32.4 us -> none  [per_device(): lax.all_gather(heads, 'dp', axis=0, tiled=True)]
    all_to_all x1 -> x0, starting transfers between devices: 11.6 us -> none  [per_device(): lax.all_to_all(normed, 'dp', split_axis=1, concat_axis=0, tiled=True)]
    all_to_all x1 -> x0, waiting for transfers between devices: 10.9 us -> none  [per_device(): lax.all_to_all(normed, 'dp', split_axis=1, concat_axis=0, tiled=True)]
    gather x2 -> x0, local copies, waits for them, and re-layouts: 10.5 us -> none  [the longest x1 5.26 us: per_device(): values = jnp.take(value_cache[:, 0], local, axis=0)]
    ppermute x5 -> x3, starting transfers between devices: 12 us -> 3.25 us  [the longest x2 2.79 us: core_swap(): return lax.ppermute(value, 'tensor', [(t, t ^ 1) for t in range(16)])]
  transfers between devices with their start and end apart: 7 -> 3, of which waited for: 4 -> 3; matrix products, arithmetic and copies ran while one was open for 4% -> 0% of each run, Pallas kernels for 0% -> 0%
where the time goes in v2:
time: 100 us; the launch traced here: 99.9 us
  blocking collectives  83.6 us (84%)
  Pallas kernels  6.05 us (6%)
  waiting for transfers between devices  4.91 us (5%)
  starting transfers between devices  3.25 us (3%)
  matrix products  1.12 us (1%)
    all_to_all x3, blocking collectives, exchange(): lax.all_to_all(value, ('dp', 'tensor'), 0, 0, tiled=True, axis_index_grou...  52.4 us
    all_to_all x1, blocking collectives, per_device(): lax.all_to_all(partial.astype(jnp.float16).reshape(blocks, rows, cols + h...  16.1 us
    all_to_all x1, blocking collectives, per_device(): spread_heads = lax.all_to_all(copies, 'dp', 0, 0, tiled=True)  15.1 us
    pallas_call x1, Pallas kernels, per_device(): pl.pallas_call(attention_kernel, out_shape=(shape, shape), in_specs=[SMEM...  4.48 us
    ppermute x1, waiting for transfers between devices, per_device(): block = lax.ppermute(block, ('dp', 'tensor'), MOVES)  3.1 us
    ppermute x2, starting transfers between devices, core_swap(): return lax.ppermute(value, 'tensor', [(t, t ^ 1) for t in range(16)])  2.79 us
  transfers between devices with their start and end apart: 3, of which 3 were waited for; matrix products, arithmetic and copies ran while one was open for 0% of the time, Pallas kernels for 0%

profile of v2, /device:TPU:1, one launch (start us, length us, event | category | flops | bytes accessed | tf_op | source)
XLA Modules:
  0.0 99.9 jit_solution(7744188609118644892)
XLA Ops:
  0.0 1.4 %shard_map.91 = (bf16[16,8,1024]{2,1,0:T(8,128)(2,1)S(1)}, bf16[1024,128]{1,0:T(8,128)(2,1)S(1)}, f32[8,128]{1,0:T(8,128)S(1)}, f32[8,128]{1,0:T(8,128)S(1)}, f3...) custom-call(bf16[8,16384]{1,0:T(8,128)(2,1)} %hidden_hbm.1, f32[1,16384]{1,0:T(1,128)} %bitcast.19, ...), custom_call_target="tpu_custom_call" | custom-call | tf_op jit(solution)/shard_map/pallas_call | solution.py:185
  1.4 23.0 %all_to_all.25 = bf16[16,8,1024]{2,1,0:T(8,128)(2,1)S(1)} all-to-all(bf16[16,8,1024]{2,1,0:T(8,128)(2,1)S(1)} %get-tuple-element.13), channel_id=1, replica_groups={{0,16,34,50,64,80,98,114,128,144,162,178,192,208,226,242},{1,17,35,51,6..., dimensions={0} | all-to-all | bytes 524288 | tf_op jit(solution)/shard_map/all_to_all | solution.py:41
  24.4 0.2 fusion.5
  24.7 0.0 copy-start.1
  24.7 0.0 copy-start.2
  24.7 0.0 copy-start.3
  24.7 0.4 fusion
  25.1 0.1 fusion.3
  25.2 16.1 %all_to_all.26 = f16[16,8,1152]{2,1,0:T(8,128)(2,1)S(1)} all-to-all(f16[16,8,1152]{2,1,0:T(8,128)(2,1)S(1)} %fusion.3), channel_id=1, replica_groups=mesh['dp'=16,'tensor'=16] {'dp'}, dimensions={0} | all-to-all | bytes 589824 | tf_op jit(solution)/shard_map/all_to_all | solution.py:206
  41.4 0.1 shard_map.92.own
  41.5 0.0 copy-start.4
  41.5 2.4 %collective-permute-start = (bf16[8,16,128]{2,1,0:T(8,128)(2,1)S(1)}, bf16[8,16,128]{2,1,0:T(8,128)(2,1)S(1)}, u32[]{:S(2)}, u32[]{:S(2)}) collective-permute-start(bf16[8,16,128]{2,1,0:T(8,128)(2,1)S(1)} %shard_map.92.own), channel_id=1, source_target_pairs={{0,1},{1,0},{2,3},{3,2},{4,5},{5,4},{6,7},{7,6},{8,9},{9,8},{10,11... | collective-permute-start | bytes 98312 | tf_op jit(solution)/shard_map/ppermute | solution.py:51
  43.8 0.9 collective-permute-done.other
  44.7 4.5 %shard_map.93 = (f32[8,8,384]{2,1,0:T(8,128)S(1)}, f32[8,8,384]{2,1,0:T(8,128)S(1)}) custom-call(s32[8]{0:T(128)S(1)} %copy-done.3, s32[8]{0:T(128)S(1)} %copy-done.2, bf16[8,16,128]{2,1,0:T(8,128)(2,1)S(1)} %shard_map.92.own, bf16[8,16,128]{2,1,0:T(8,128)(2,1)S(1)} %collective-permute-done.other, bf16[8,1,2048,128]{3,2,1,0:T(8,128)(2,1)S(1)} %copy-done.1, ...), custom_call_target="tpu_custom_call" | custom-call | tf_op jit(solution)/shard_map/pallas_call | solution.py:219
  49.2 0.4 collective-permute-start.1
  49.6 0.9 collective-permute-done.1.theirs
  50.6 0.1 shard_map.94
  50.6 15.1 %all_to_all.27 = bf16[16,8,1024]{2,1,0:T(8,128)(2,1)S(1)} all-to-all(bf16[16,8,1024]{2,1,0:T(8,128)(2,1)S(1)} %shard_map.94), channel_id=1, replica_groups=mesh['dp'=16,'tensor'=16] {'dp'}, dimensions={0} | all-to-all | bytes 524288 | tf_op jit(solution)/shard_map/all_to_all | solution.py:239
  65.7 0.5 fusion.2
  66.2 13.1 %all_to_all.28 = bf16[16,8,1024]{2,1,0:T(8,128)(2,1)S(1)} all-to-all(bf16[16,8,1024]{2,1,0:T(8,128)(2,1)S(1)} %fusion.2), channel_id=1, replica_groups={{0,1,2,3,4,5,6,7,8,9,10,11,12,13,14,15},{17,16,19,18,21,20,23,22,25,24,..., dimensions={0} | all-to-all | bytes 524288 | tf_op jit(solution)/shard_map/all_to_all | solution.py:41
  79.3 0.5 collective-permute-start.2
  79.8 3.1 %collective-permute-done.2 = bf16[8,1024]{1,0:T(8,128)(2,1)S(1)} collective-permute-done((bf16[8,1024]{1,0:T(8,128)(2,1)S(1)}, bf16[8,1024]{1,0:T(8,128)(2,1)S(1)}, u32[]{:S(2)}, u32[]{:S(2)}) %collective-permute-start.2) | collective-permute-done | bytes 16416 | tf_op jit(solution)/shard_map/ppermute | solution.py:245
  82.9 16.3 %all_to_all.29 = bf16[16,8,1024]{2,1,0:T(8,128)(2,1)S(1)} all-to-all(bf16[16,8,1024]{2,1,0:T(8,128)(2,1)S(1)} %broadcast_in_dim.10), channel_id=1, replica_groups={{2,1,0,3,6,5,4,7,10,9,8,11,14,13,12,15},{17,18,19,16,21,22,23,20,25,26,..., dimensions={0} | all-to-all | bytes 524288 | tf_op jit(solution)/shard_map/all_to_all | solution.py:41
  99.2 0.7 copy.11
  (10 shorter events, 0.1 us)
Async XLA Ops:
  0.0 24.7 %copy-start = (bf16[1024,1024]{1,0:T(8,128)(2,1)S(1)}, bf16[1024,1024]{1,0:T(8,128)(2,1)}, u32[]{:S(2)}) copy-start(bf16[1024,1024]{1,0:T(8,128)(2,1)} %param.11) | copy-start | bytes 6291460
  24.7 20.0 %copy-start.1 = (bf16[8,1,2048,128]{3,2,1,0:T(8,128)(2,1)S(1)}, bf16[8,1,2048,128]{3,2,1,0:T(8,128)(2,1)}, u32[]{:S(2)}) copy-start(bf16[8,1,2048,128]{3,2,1,0:T(8,128)(2,1)} %keys.1) | copy-start | bytes 12582916
  24.7 20.0 %copy-start.2 = (s32[8]{0:T(128)S(1)}, s32[8]{0:T(128)}, u32[]{:S(2)}) copy-start(s32[8]{0:T(128)} %lengths.1) | copy-start | bytes 100
  24.7 20.0 %copy-start.3 = (s32[8]{0:T(128)S(1)}, s32[8]{0:T(128)}, u32[]{:S(2)}) copy-start(s32[8]{0:T(128)} %parent.1) | copy-start | bytes 100
  41.5 24.3 %copy-start.4 = (bf16[1024,1024]{1,0:T(8,128)(2,1)S(1)}, bf16[1024,1024]{1,0:T(8,128)(2,1)}, u32[]{:S(2)}) copy-start(bf16[1024,1024]{1,0:T(8,128)(2,1)} %param.13) | copy-start | bytes 6291460
  41.5 3.2 %collective-permute-start = (bf16[8,16,128]{2,1,0:T(8,128)(2,1)S(1)}, bf16[8,16,128]{2,1,0:T(8,128)(2,1)S(1)}, u32[]{:S(2)}, u32[]{:S(2)}) collective-permute-start(bf16[8,16,128]{2,1,0:T(8,128)(2,1)S(1)} %shard_map.92.own), channel_id=1, source_target_pairs={{0,1},{1,0},{2,3},{3,2},{4,5},{5,4},{6,7},{7,6},{8,9},{9,8},{10,11... | collective-permute-start | bytes 98312 | tf_op jit(solution)/shard_map/ppermute | solution.py:51
  49.2 1.4 %collective-permute-start.1 = (f32[8,8,384]{2,1,0:T(8,128)S(1)}, f32[8,8,384]{2,1,0:T(8,128)S(1)}, u32[]{:S(2)}, u32[]{:S(2)}) collective-permute-start(f32[8,8,384]{2,1,0:T(8,128)S(1)} %get-tuple-element.20), channel_id=1, source_target_pairs={{0,1},{1,0},{2,3},{3,2},{4,5},{5,4},{6,7},{7,6},{8,9},{9,8},{10,11... | collective-permute-start | bytes 294920 | tf_op jit(solution)/shard_map/ppermute | solution.py:51
  79.3 3.6 %collective-permute-start.2 = (bf16[8,1024]{1,0:T(8,128)(2,1)S(1)}, bf16[8,1024]{1,0:T(8,128)(2,1)S(1)}, u32[]{:S(2)}, u32[]{:S(2)}) collective-permute-start(bf16[8,1024]{1,0:T(8,128)(2,1)S(1)} %reduce_sum.22), channel_id=1, source_target_pairs={{0,2},{1,17},{2,32},{3,51},{4,70},{5,85},{6,100},{7,119},{8,138},{... | collective-permute-start | bytes 49160 | tf_op jit(solution)/shard_map/ppermute | solution.py:245

commit v3 on v2

--- a/solution.py
+++ b/solution.py
@@ -94,7 +94,7 @@
     copies[3].wait()
 
 
-def rotate_kernel(total, cosine, sine, kv_cosine, kv_sine, out, turned):
+def rotate_kernel(total, cosine, sine, kv_cosine, kv_sine, values, out, turned):
     heads = total.shape[1] // 128 - 1
     for h in range(heads + 1):
         t = total[:, h * 128 : (h + 1) * 128]
@@ -108,18 +108,11 @@
 
 
 def attention_kernel(
-    parent, lengths, own, other, keys, value_cache, keep, send, values, weights, sems
+    parent, lengths, own, other, keys, values, keep, send, weights
 ):
     rows, _, half, hd = keys.shape
     base = lax.axis_index("dp") * rows
     parity = lax.axis_index("tensor") % 2
-    copies = []
-    for r in range(rows):
-        src = parent[r] - base
-        copies.append(
-            pltpu.make_async_copy(value_cache.at[src, 0], values.at[r], sems.at[r])
-        )
-        copies[r].start()
     scale = hd ** (-0.5)
     second = parity == 1
     column = lax.broadcasted_iota(jnp.int32, (16, half), 1)
@@ -147,11 +140,9 @@
         weights[r] = weight.astype(jnp.bfloat16)
         added = newweight.astype(jnp.bfloat16).astype(jnp.float32) * new_value
         found.append((added, top, total))
-    for copy in copies:
-        copy.wait()
     for r in range(rows):
         added, top, total = found[r]
-        acc = jnp.dot(weights[r], values[r], preferred_element_type=jnp.float32) + added
+        acc = jnp.dot(weights[r], values[parent[r] - base, 0], preferred_element_type=jnp.float32) + added
         top = jnp.broadcast_to(top, acc.shape)
         total = jnp.broadcast_to(total, acc.shape)
         for k, part in enumerate((acc, top, total)):
@@ -209,25 +200,23 @@
     own = pl.pallas_call(
         rotate_kernel,
         out_shape=jax.ShapeDtypeStruct((rows, 16, hd), jnp.bfloat16),
-        in_specs=[VMEM] * 5,
+        in_specs=[VMEM] * 6,
         out_specs=VMEM,
         scratch_shapes=[pltpu.VMEM((rows, 16, hd), jnp.float32)],
         compiler_params=pltpu.CompilerParams(vmem_limit_bytes=8 * 2**20),
-    )(jnp.sum(parts, axis=0) * (1.0 / SCALE), *tables)
+            )(jnp.sum(parts, axis=0) * (1.0 / SCALE), *tables, value_cache)
     other = core_swap(own)
     shape = jax.ShapeDtypeStruct((heads, rows, 3 * hd), jnp.float32)
     keep, send = pl.pallas_call(
         attention_kernel,
         out_shape=(shape, shape),
-        in_specs=[SMEM, SMEM, VMEM, VMEM, VMEM, HBM],
+        in_specs=[SMEM, SMEM, VMEM, VMEM, VMEM, VMEM],
         out_specs=(VMEM, VMEM),
         scratch_shapes=[
-            pltpu.VMEM((rows, half, hd), jnp.bfloat16),
             pltpu.VMEM((rows, 2 * heads, half), jnp.bfloat16),
-            pltpu.SemaphoreType.DMA((rows,)),
         ],
         compiler_params=pltpu.CompilerParams(vmem_limit_bytes=24 * 2**20),
-    )(parent, lengths, own, other, key_cache, in_hbm(value_cache))
+    )(parent, lengths, own, other, key_cache, value_cache)
     received = core_swap(send)
     copies = pl.pallas_call(
         merge_kernel,

time: 100 us -> 99.3 us (level)
  Pallas kernels: 6.05 us -> 3.99 us
    pallas_call x1, Pallas kernels: 4.48 us -> 2.42 us  [per_device(): pl.pallas_call(attention_kernel, out_shape=(shape, shape), in_specs=[SMEM...]
where the time goes in v3:
time: 99.3 us; the launch traced here: 99.1 us
  blocking collectives  84 us (85%)
  waiting for transfers between devices  5.28 us (5%)
  Pallas kernels  3.99 us (4%)
  starting transfers between devices  3.61 us (4%)
  matrix products  1.12 us (1%)
    all_to_all x3, blocking collectives, exchange(): lax.all_to_all(value, ('dp', 'tensor'), 0, 0, tiled=True, axis_index_grou...  52.8 us
    all_to_all x1, blocking collectives, per_device(): lax.all_to_all(partial.astype(jnp.float16).reshape(blocks, rows, cols + h...  16.1 us
    all_to_all x1, blocking collectives, per_device(): spread_heads = lax.all_to_all(copies, 'dp', 0, 0, tiled=True)  15.2 us
    ppermute x2, starting transfers between devices, core_swap(): return lax.ppermute(value, 'tensor', [(t, t ^ 1) for t in range(16)])  3.53 us
    ppermute x1, waiting for transfers between devices, per_device(): block = lax.ppermute(block, ('dp', 'tensor'), MOVES)  3.47 us
    pallas_call x1, Pallas kernels, per_device(): pl.pallas_call(attention_kernel, out_shape=(shape, shape), in_specs=[SMEM...  2.42 us
  transfers between devices with their start and end apart: 3, of which 3 were waited for; matrix products, arithmetic and copies ran while one was open for 0% of the time, Pallas kernels for 0%

profile of v3, /device:TPU:1, one launch (start us, length us, event | category | flops | bytes accessed | tf_op | source)
XLA Modules:
  0.0 99.1 jit_solution(12730257360304215560)
XLA Ops:
  0.0 1.4 %shard_map.91 = (bf16[16,8,1024]{2,1,0:T(8,128)(2,1)S(1)}, bf16[1024,128]{1,0:T(8,128)(2,1)S(1)}, f32[8,128]{1,0:T(8,128)S(1)}, f32[8,128]{1,0:T(8,128)S(1)}, f3...) custom-call(bf16[8,16384]{1,0:T(8,128)(2,1)} %hidden_hbm.1, f32[1,16384]{1,0:T(1,128)} %bitcast.19, ...), custom_call_target="tpu_custom_call" | custom-call | tf_op jit(solution)/shard_map/pallas_call | solution.py:176
  1.4 23.0 %all_to_all.25 = bf16[16,8,1024]{2,1,0:T(8,128)(2,1)S(1)} all-to-all(bf16[16,8,1024]{2,1,0:T(8,128)(2,1)S(1)} %get-tuple-element.13), channel_id=1, replica_groups={{0,16,34,50,64,80,98,114,128,144,162,178,192,208,226,242},{1,17,35,51,6..., dimensions={0} | all-to-all | bytes 524288 | tf_op jit(solution)/shard_map/all_to_all | solution.py:41
  24.4 0.2 fusion.5
  24.7 0.0 copy-start.1
  24.7 0.4 fusion
  25.1 0.1 fusion.3
  25.2 16.1 %all_to_all.26 = f16[16,8,1152]{2,1,0:T(8,128)(2,1)S(1)} all-to-all(f16[16,8,1152]{2,1,0:T(8,128)(2,1)S(1)} %fusion.3), channel_id=1, replica_groups=mesh['dp'=16,'tensor'=16] {'dp'}, dimensions={0} | all-to-all | bytes 589824 | tf_op jit(solution)/shard_map/all_to_all | solution.py:197
  41.3 0.0 copy-start.3
  41.4 0.0 copy-start.4
  41.4 0.1 shard_map.92.own
  41.5 0.0 copy-start.5
  41.5 2.4 %collective-permute-start = (bf16[8,16,128]{2,1,0:T(8,128)(2,1)S(1)}, bf16[8,16,128]{2,1,0:T(8,128)(2,1)S(1)}, u32[]{:S(2)}, u32[]{:S(2)}) collective-permute-start(bf16[8,16,128]{2,1,0:T(8,128)(2,1)S(1)} %shard_map.92.own), channel_id=1, source_target_pairs={{0,1},{1,0},{2,3},{3,2},{4,5},{5,4},{6,7},{7,6},{8,9},{9,8},{10,11... | collective-permute-start | bytes 98312 | tf_op jit(solution)/shard_map/ppermute | solution.py:51
  43.8 0.9 collective-permute-done.other
  44.7 2.4 %shard_map.93 = (f32[8,8,384]{2,1,0:T(8,128)S(1)}, f32[8,8,384]{2,1,0:T(8,128)S(1)}) custom-call(s32[8]{0:T(128)S(1)} %copy-done.4, s32[8]{0:T(128)S(1)} %copy-done.3, bf16[8,16,128]{2,1,0:T(8,128)(2,1)S(1)} %shard_map.92.own, bf16[8,16,128]{2,1,0:T(8,128)(2,1)S(1)} %collective-permute-done.other, bf16[8,1,2048,128]{3,2,1,0:T(8,128)(2,1)S(1)} %copy-done.2, ...), custom_call_target="tpu_custom_call" | custom-call | tf_op jit(solution)/shard_map/pallas_call | solution.py:210
  47.1 1.2 %collective-permute-start.1 = (f32[8,8,384]{2,1,0:T(8,128)S(1)}, f32[8,8,384]{2,1,0:T(8,128)S(1)}, u32[]{:S(2)}, u32[]{:S(2)}) collective-permute-start(f32[8,8,384]{2,1,0:T(8,128)S(1)} %get-tuple-element.20), channel_id=1, source_target_pairs={{0,1},{1,0},{2,3},{3,2},{4,5},{5,4},{6,7},{7,6},{8,9},{9,8},{10,11... | collective-permute-start | bytes 294920 | tf_op jit(solution)/shard_map/ppermute | solution.py:51
  48.3 0.9 collective-permute-done.1.theirs
  49.3 0.1 shard_map.94
  49.3 15.2 %all_to_all.27 = bf16[16,8,1024]{2,1,0:T(8,128)(2,1)S(1)} all-to-all(bf16[16,8,1024]{2,1,0:T(8,128)(2,1)S(1)} %shard_map.94), channel_id=1, replica_groups=mesh['dp'=16,'tensor'=16] {'dp'}, dimensions={0} | all-to-all | bytes 524288 | tf_op jit(solution)/shard_map/all_to_all | solution.py:228
  64.5 0.5 fusion.2
  65.0 13.5 %all_to_all.28 = bf16[16,8,1024]{2,1,0:T(8,128)(2,1)S(1)} all-to-all(bf16[16,8,1024]{2,1,0:T(8,128)(2,1)S(1)} %fusion.2), channel_id=1, replica_groups={{0,1,2,3,4,5,6,7,8,9,10,11,12,13,14,15},{17,16,19,18,21,20,23,22,25,24,..., dimensions={0} | all-to-all | bytes 524288 | tf_op jit(solution)/shard_map/all_to_all | solution.py:41
  78.5 0.1 collective-permute-start.2
  78.6 3.5 %collective-permute-done.2 = bf16[8,1024]{1,0:T(8,128)(2,1)S(1)} collective-permute-done((bf16[8,1024]{1,0:T(8,128)(2,1)S(1)}, bf16[8,1024]{1,0:T(8,128)(2,1)S(1)}, u32[]{:S(2)}, u32[]{:S(2)}) %collective-permute-start.2) | collective-permute-done | bytes 16416 | tf_op jit(solution)/shard_map/ppermute | solution.py:234
  82.1 16.3 %all_to_all.29 = bf16[16,8,1024]{2,1,0:T(8,128)(2,1)S(1)} all-to-all(bf16[16,8,1024]{2,1,0:T(8,128)(2,1)S(1)} %broadcast_in_dim.10), channel_id=1, replica_groups={{2,1,0,3,6,5,4,7,10,9,8,11,14,13,12,15},{17,18,19,16,21,22,23,20,25,26,..., dimensions={0} | all-to-all | bytes 524288 | tf_op jit(solution)/shard_map/all_to_all | solution.py:41
  98.4 0.7 copy.11
  (12 shorter events, 0.1 us)
Async XLA Ops:
  0.0 24.6 %copy-start = (bf16[1024,1024]{1,0:T(8,128)(2,1)S(1)}, bf16[1024,1024]{1,0:T(8,128)(2,1)}, u32[]{:S(2)}) copy-start(bf16[1024,1024]{1,0:T(8,128)(2,1)} %param.11) | copy-start | bytes 6291460
  24.7 16.7 %copy-start.1 = (bf16[8,1,2048,128]{3,2,1,0:T(8,128)(2,1)S(1)}, bf16[8,1,2048,128]{3,2,1,0:T(8,128)(2,1)}, u32[]{:S(2)}) copy-start(bf16[8,1,2048,128]{3,2,1,0:T(8,128)(2,1)} %values.3) | copy-start | bytes 12582916
  41.3 3.4 %copy-start.2 = (bf16[8,1,2048,128]{3,2,1,0:T(8,128)(2,1)S(1)}, bf16[8,1,2048,128]{3,2,1,0:T(8,128)(2,1)}, u32[]{:S(2)}) copy-start(bf16[8,1,2048,128]{3,2,1,0:T(8,128)(2,1)} %keys.1) | copy-start | bytes 12582916
  41.3 3.4 %copy-start.3 = (s32[8]{0:T(128)S(1)}, s32[8]{0:T(128)}, u32[]{:S(2)}) copy-start(s32[8]{0:T(128)} %lengths.1) | copy-start | bytes 100
  41.4 3.4 %copy-start.4 = (s32[8]{0:T(128)S(1)}, s32[8]{0:T(128)}, u32[]{:S(2)}) copy-start(s32[8]{0:T(128)} %parent.1) | copy-start | bytes 100
  41.5 23.0 %copy-start.5 = (bf16[1024,1024]{1,0:T(8,128)(2,1)S(1)}, bf16[1024,1024]{1,0:T(8,128)(2,1)}, u32[]{:S(2)}) copy-start(bf16[1024,1024]{1,0:T(8,128)(2,1)} %param.13) | copy-start | bytes 6291460
  41.5 3.2 %collective-permute-start = (bf16[8,16,128]{2,1,0:T(8,128)(2,1)S(1)}, bf16[8,16,128]{2,1,0:T(8,128)(2,1)S(1)}, u32[]{:S(2)}, u32[]{:S(2)}) collective-permute-start(bf16[8,16,128]{2,1,0:T(8,128)(2,1)S(1)} %shard_map.92.own), channel_id=1, source_target_pairs={{0,1},{1,0},{2,3},{3,2},{4,5},{5,4},{6,7},{7,6},{8,9},{9,8},{10,11... | collective-permute-start | bytes 98312 | tf_op jit(solution)/shard_map/ppermute | solution.py:51
  47.1 2.1 %collective-permute-start.1 = (f32[8,8,384]{2,1,0:T(8,128)S(1)}, f32[8,8,384]{2,1,0:T(8,128)S(1)}, u32[]{:S(2)}, u32[]{:S(2)}) collective-permute-start(f32[8,8,384]{2,1,0:T(8,128)S(1)} %get-tuple-element.20), channel_id=1, source_target_pairs={{0,1},{1,0},{2,3},{3,2},{4,5},{5,4},{6,7},{7,6},{8,9},{9,8},{10,11... | collective-permute-start | bytes 294920 | tf_op jit(solution)/shard_map/ppermute | solution.py:51
  78.5 3.6 %collective-permute-start.2 = (bf16[8,1024]{1,0:T(8,128)(2,1)S(1)}, bf16[8,1024]{1,0:T(8,128)(2,1)S(1)}, u32[]{:S(2)}, u32[]{:S(2)}) collective-permute-start(bf16[8,1024]{1,0:T(8,128)(2,1)S(1)} %reduce_sum.22), channel_id=1, source_target_pairs={{0,2},{1,17},{2,32},{3,51},{4,70},{5,85},{6,100},{7,119},{8,138},{... | collective-permute-start | bytes 49160 | tf_op jit(solution)/shard_map/ppermute | solution.py:234

commit v4 on v3

--- a/solution.py
+++ b/solution.py
@@ -26,15 +26,23 @@
 ]
 
 
-def holder(j, t):
-    return t ^ 2 if t % 4 in (0, 2) else t
-
-
-SUM_GROUPS = [[j * 16 + (j ^ p) for p in range(16)] for j in range(16)]
+X_MOVES = (2, 1, 0, 3)
+Z_MOVES = {(1, 0): (1, 0), (0, 0): (3, 1), (0, 1): (2, 1), (1, 1): (0, 0)}
+
+
+def target(j, t):
+    y, z_lo, core = t // 4, t // 2 % 2, t % 2
+    z_move, z_lo = Z_MOVES[z_lo, core]
+    x, z_hi = (j // 4 + X_MOVES[y]) % 4, (j % 4 + z_move) % 4
+    return x * 4 + z_hi, y * 4 + z_lo * 2 + core
+
+
+SUMMER = {(j, target(j, t)[0]): t for j in range(16) for t in range(16)}
+SUM_GROUPS = [[j * 16 + SUMMER[j, p] for p in range(16)] for j in range(16)]
 MOVES = [
-    (j * 16 + t, (j ^ t) * 16 + holder(j, t)) for j in range(16) for t in range(16)
+    (j * 16 + t, target(j, t)[0] * 16 + target(j, t)[1]) for j in range(16) for t in range(16)
 ]
-WHOLE_GROUPS = [[i * 16 + holder(p, i ^ p) for p in range(16)] for i in range(16)]
+WHOLE_GROUPS = [[i * 16 + target(p, SUMMER[p, i])[1] for p in range(16)] for i in range(16)]
 
 
 def exchange(value, groups):

time: 99.3 us -> 95.5 us (0.962)
  blocking collectives: 84 us -> 78.7 us
  starting transfers between devices: 3.61 us -> 5.82 us
    all_to_all x3, blocking collectives: 52.8 us -> 47.5 us  [exchange(): lax.all_to_all(value, ('dp', 'tensor'), 0, 0, tiled=True, axis_index_grou...]
    ppermute x1, starting transfers between devices: 0.08 us -> 2.3 us  [per_device(): block = lax.ppermute(block, ('dp', 'tensor'), MOVES)]
where the time goes in v4:
time: 95.5 us; the launch traced here: 95.3 us
  blocking collectives  78.7 us (82%)
  starting transfers between devices  5.82 us (6%)
  waiting for transfers between devices  4.57 us (5%)
  Pallas kernels  3.99 us (4%)
  matrix products  1.12 us (1%)
    all_to_all x3, blocking collectives, exchange(): lax.all_to_all(value, ('dp', 'tensor'), 0, 0, tiled=True, axis_index_grou...  47.5 us
    all_to_all x1, blocking collectives, per_device(): lax.all_to_all(partial.astype(jnp.float16).reshape(blocks, rows, cols + h...  16.1 us
    all_to_all x1, blocking collectives, per_device(): spread_heads = lax.all_to_all(copies, 'dp', 0, 0, tiled=True)  15.2 us
    ppermute x2, starting transfers between devices, core_swap(): return lax.ppermute(value, 'tensor', [(t, t ^ 1) for t in range(16)])  3.53 us
    ppermute x1, waiting for transfers between devices, per_device(): block = lax.ppermute(block, ('dp', 'tensor'), MOVES)  2.77 us
    pallas_call x1, Pallas kernels, per_device(): pl.pallas_call(attention_kernel, out_shape=(shape, shape), in_specs=[SMEM...  2.42 us
    ppermute x1, starting transfers between devices, per_device(): block = lax.ppermute(block, ('dp', 'tensor'), MOVES)  2.3 us
  transfers between devices with their start and end apart: 3, of which 3 were waited for; matrix products, arithmetic and copies ran while one was open for 0% of the time, Pallas kernels for 0%

profile of v4, /device:TPU:1, one launch (start us, length us, event | category | flops | bytes accessed | tf_op | source)
XLA Modules:
  0.0 95.3 jit_solution(13450733833792400888)
XLA Ops:
  0.0 1.4 %shard_map.91 = (bf16[16,8,1024]{2,1,0:T(8,128)(2,1)S(1)}, bf16[1024,128]{1,0:T(8,128)(2,1)S(1)}, f32[8,128]{1,0:T(8,128)S(1)}, f32[8,128]{1,0:T(8,128)S(1)}, f3...) custom-call(bf16[8,16384]{1,0:T(8,128)(2,1)} %hidden_hbm.1, f32[1,16384]{1,0:T(1,128)} %bitcast.19, ...), custom_call_target="tpu_custom_call" | custom-call | tf_op jit(solution)/shard_map/pallas_call | solution.py:184
  1.4 23.0 %all_to_all.25 = bf16[16,8,1024]{2,1,0:T(8,128)(2,1)S(1)} all-to-all(bf16[16,8,1024]{2,1,0:T(8,128)(2,1)S(1)} %get-tuple-element.13), channel_id=1, replica_groups={{0,16,34,50,64,80,98,114,128,144,162,178,192,208,226,242},{1,17,35,51,6..., dimensions={0} | all-to-all | bytes 524288 | tf_op jit(solution)/shard_map/all_to_all | solution.py:49
  24.4 0.2 fusion.5
  24.7 0.0 copy-start.1
  24.7 0.4 fusion
  25.1 0.1 fusion.3
  25.2 16.1 %all_to_all.26 = f16[16,8,1152]{2,1,0:T(8,128)(2,1)S(1)} all-to-all(f16[16,8,1152]{2,1,0:T(8,128)(2,1)S(1)} %fusion.3), channel_id=1, replica_groups=mesh['dp'=16,'tensor'=16] {'dp'}, dimensions={0} | all-to-all | bytes 589824 | tf_op jit(solution)/shard_map/all_to_all | solution.py:205
  41.3 0.0 copy-start.3
  41.4 0.0 copy-start.4
  41.4 0.1 shard_map.92.own
  41.5 0.0 copy-start.5
  41.5 2.4 %collective-permute-start = (bf16[8,16,128]{2,1,0:T(8,128)(2,1)S(1)}, bf16[8,16,128]{2,1,0:T(8,128)(2,1)S(1)}, u32[]{:S(2)}, u32[]{:S(2)}) collective-permute-start(bf16[8,16,128]{2,1,0:T(8,128)(2,1)S(1)} %shard_map.92.own), channel_id=1, source_target_pairs={{0,1},{1,0},{2,3},{3,2},{4,5},{5,4},{6,7},{7,6},{8,9},{9,8},{10,11... | collective-permute-start | bytes 98312 | tf_op jit(solution)/shard_map/ppermute | solution.py:59
  43.8 0.9 collective-permute-done.other
  44.7 2.4 %shard_map.93 = (f32[8,8,384]{2,1,0:T(8,128)S(1)}, f32[8,8,384]{2,1,0:T(8,128)S(1)}) custom-call(s32[8]{0:T(128)S(1)} %copy-done.4, s32[8]{0:T(128)S(1)} %copy-done.3, bf16[8,16,128]{2,1,0:T(8,128)(2,1)S(1)} %shard_map.92.own, bf16[8,16,128]{2,1,0:T(8,128)(2,1)S(1)} %collective-permute-done.other, bf16[8,1,2048,128]{3,2,1,0:T(8,128)(2,1)S(1)} %copy-done.2, ...), custom_call_target="tpu_custom_call" | custom-call | tf_op jit(solution)/shard_map/pallas_call | solution.py:218
  47.1 1.2 %collective-permute-start.1 = (f32[8,8,384]{2,1,0:T(8,128)S(1)}, f32[8,8,384]{2,1,0:T(8,128)S(1)}, u32[]{:S(2)}, u32[]{:S(2)}) collective-permute-start(f32[8,8,384]{2,1,0:T(8,128)S(1)} %get-tuple-element.20), channel_id=1, source_target_pairs={{0,1},{1,0},{2,3},{3,2},{4,5},{5,4},{6,7},{7,6},{8,9},{9,8},{10,11... | collective-permute-start | bytes 294920 | tf_op jit(solution)/shard_map/ppermute | solution.py:59
  48.3 0.9 collective-permute-done.1.theirs
  49.3 0.1 shard_map.94
  49.3 15.2 %all_to_all.27 = bf16[16,8,1024]{2,1,0:T(8,128)(2,1)S(1)} all-to-all(bf16[16,8,1024]{2,1,0:T(8,128)(2,1)S(1)} %shard_map.94), channel_id=1, replica_groups=mesh['dp'=16,'tensor'=16] {'dp'}, dimensions={0} | all-to-all | bytes 524288 | tf_op jit(solution)/shard_map/all_to_all | solution.py:236
  64.5 0.5 fusion.2
  65.0 11.4 %all_to_all.28 = bf16[16,8,1024]{2,1,0:T(8,128)(2,1)S(1)} all-to-all(bf16[16,8,1024]{2,1,0:T(8,128)(2,1)S(1)} %fusion.2), channel_id=1, replica_groups={{11,10,9,8,7,6,5,4,3,2,1,0,15,14,13,12},{24,27,26,25,20,23,22,21,16,19,..., dimensions={0} | all-to-all | bytes 524288 | tf_op jit(solution)/shard_map/all_to_all | solution.py:49
  76.4 2.3 %collective-permute-start.2 = (bf16[8,1024]{1,0:T(8,128)(2,1)S(1)}, bf16[8,1024]{1,0:T(8,128)(2,1)S(1)}, u32[]{:S(2)}, u32[]{:S(2)}) collective-permute-start(bf16[8,1024]{1,0:T(8,128)(2,1)S(1)} %reduce_sum.22), channel_id=1, source_target_pairs={{0,178},{1,163},{2,144},{3,129},{4,118},{5,103},{6,84},{7,69},{8,5... | collective-permute-start | bytes 49160 | tf_op jit(solution)/shard_map/ppermute | solution.py:242
  78.7 2.8 %collective-permute-done.2 = bf16[8,1024]{1,0:T(8,128)(2,1)S(1)} collective-permute-done((bf16[8,1024]{1,0:T(8,128)(2,1)S(1)}, bf16[8,1024]{1,0:T(8,128)(2,1)S(1)}, u32[]{:S(2)}, u32[]{:S(2)}) %collective-permute-start.2) | collective-permute-done | bytes 16416 | tf_op jit(solution)/shard_map/ppermute | solution.py:242
  81.5 13.1 %all_to_all.29 = bf16[16,8,1024]{2,1,0:T(8,128)(2,1)S(1)} all-to-all(bf16[16,8,1024]{2,1,0:T(8,128)(2,1)S(1)} %broadcast_in_dim.10), channel_id=1, replica_groups={{9,10,11,8,13,14,15,12,1,2,3,0,5,6,7,4},{24,25,26,27,28,29,30,31,16,17,..., dimensions={0} | all-to-all | bytes 524288 | tf_op jit(solution)/shard_map/all_to_all | solution.py:49
  94.6 0.7 copy.11
  (12 shorter events, 0.1 us)
Async XLA Ops:
  0.0 24.6 %copy-start = (bf16[1024,1024]{1,0:T(8,128)(2,1)S(1)}, bf16[1024,1024]{1,0:T(8,128)(2,1)}, u32[]{:S(2)}) copy-start(bf16[1024,1024]{1,0:T(8,128)(2,1)} %param.11) | copy-start | bytes 6291460
  24.7 16.7 %copy-start.1 = (bf16[8,1,2048,128]{3,2,1,0:T(8,128)(2,1)S(1)}, bf16[8,1,2048,128]{3,2,1,0:T(8,128)(2,1)}, u32[]{:S(2)}) copy-start(bf16[8,1,2048,128]{3,2,1,0:T(8,128)(2,1)} %values.3) | copy-start | bytes 12582916
  41.3 3.4 %copy-start.2 = (bf16[8,1,2048,128]{3,2,1,0:T(8,128)(2,1)S(1)}, bf16[8,1,2048,128]{3,2,1,0:T(8,128)(2,1)}, u32[]{:S(2)}) copy-start(bf16[8,1,2048,128]{3,2,1,0:T(8,128)(2,1)} %keys.1) | copy-start | bytes 12582916
  41.3 3.4 %copy-start.3 = (s32[8]{0:T(128)S(1)}, s32[8]{0:T(128)}, u32[]{:S(2)}) copy-start(s32[8]{0:T(128)} %lengths.1) | copy-start | bytes 100
  41.4 3.4 %copy-start.4 = (s32[8]{0:T(128)S(1)}, s32[8]{0:T(128)}, u32[]{:S(2)}) copy-start(s32[8]{0:T(128)} %parent.1) | copy-start | bytes 100
  41.5 23.0 %copy-start.5 = (bf16[1024,1024]{1,0:T(8,128)(2,1)S(1)}, bf16[1024,1024]{1,0:T(8,128)(2,1)}, u32[]{:S(2)}) copy-start(bf16[1024,1024]{1,0:T(8,128)(2,1)} %param.13) | copy-start | bytes 6291460
  41.5 3.2 %collective-permute-start = (bf16[8,16,128]{2,1,0:T(8,128)(2,1)S(1)}, bf16[8,16,128]{2,1,0:T(8,128)(2,1)S(1)}, u32[]{:S(2)}, u32[]{:S(2)}) collective-permute-start(bf16[8,16,128]{2,1,0:T(8,128)(2,1)S(1)} %shard_map.92.own), channel_id=1, source_target_pairs={{0,1},{1,0},{2,3},{3,2},{4,5},{5,4},{6,7},{7,6},{8,9},{9,8},{10,11... | collective-permute-start | bytes 98312 | tf_op jit(solution)/shard_map/ppermute | solution.py:59
  47.1 2.1 %collective-permute-start.1 = (f32[8,8,384]{2,1,0:T(8,128)S(1)}, f32[8,8,384]{2,1,0:T(8,128)S(1)}, u32[]{:S(2)}, u32[]{:S(2)}) collective-permute-start(f32[8,8,384]{2,1,0:T(8,128)S(1)} %get-tuple-element.20), channel_id=1, source_target_pairs={{0,1},{1,0},{2,3},{3,2},{4,5},{5,4},{6,7},{7,6},{8,9},{9,8},{10,11... | collective-permute-start | bytes 294920 | tf_op jit(solution)/shard_map/ppermute | solution.py:59
  76.4 5.1 %collective-permute-start.2 = (bf16[8,1024]{1,0:T(8,128)(2,1)S(1)}, bf16[8,1024]{1,0:T(8,128)(2,1)S(1)}, u32[]{:S(2)}, u32[]{:S(2)}) collective-permute-start(bf16[8,1024]{1,0:T(8,128)(2,1)S(1)} %reduce_sum.22), channel_id=1, source_target_pairs={{0,178},{1,163},{2,144},{3,129},{4,118},{5,103},{6,84},{7,69},{8,5... | collective-permute-start | bytes 49160 | tf_op jit(solution)/shard_map/ppermute | solution.py:242

commit v5 on v4

--- a/solution.py
+++ b/solution.py
@@ -33,7 +33,8 @@
 def target(j, t):
     y, z_lo, core = t // 4, t // 2 % 2, t % 2
     z_move, z_lo = Z_MOVES[z_lo, core]
-    x, z_hi = (j // 4 + X_MOVES[y]) % 4, (j % 4 + z_move) % 4
+    x_move = X_MOVES[y] + (2 if z_move == 2 else 0)
+    x, z_hi = (j // 4 + x_move) % 4, (j % 4 + z_move) % 4
     return x * 4 + z_hi, y * 4 + z_lo * 2 + core
 
 

time: 95.5 us -> 95 us (level)
  starting transfers between devices: 5.82 us -> 4.54 us
  waiting for transfers between devices: 4.57 us -> 5.85 us
    ppermute x1, waiting for transfers between devices: 2.77 us -> 4.05 us  [per_device(): block = lax.ppermute(block, ('dp', 'tensor'), MOVES)]
    ppermute x1, starting transfers between devices: 2.3 us -> 1.02 us  [per_device(): block = lax.ppermute(block, ('dp', 'tensor'), MOVES)]
where the time goes in v5:
time: 95 us; the launch traced here: 94.7 us
  blocking collectives  78.2 us (82%)
  waiting for transfers between devices  5.85 us (6%)
  starting transfers between devices  4.54 us (5%)
  Pallas kernels  3.99 us (4%)
  matrix products  1.12 us (1%)
    all_to_all x3, blocking collectives, exchange(): lax.all_to_all(value, ('dp', 'tensor'), 0, 0, tiled=True, axis_index_grou...  46.9 us
    all_to_all x1, blocking collectives, per_device(): lax.all_to_all(partial.astype(jnp.float16).reshape(blocks, rows, cols + h...  16.1 us
    all_to_all x1, blocking collectives, per_device(): spread_heads = lax.all_to_all(copies, 'dp', 0, 0, tiled=True)  15.2 us
    ppermute x1, waiting for transfers between devices, per_device(): block = lax.ppermute(block, ('dp', 'tensor'), MOVES)  4.05 us
    ppermute x2, starting transfers between devices, core_swap(): return lax.ppermute(value, 'tensor', [(t, t ^ 1) for t in range(16)])  3.53 us
    pallas_call x1, Pallas kernels, per_device(): pl.pallas_call(attention_kernel, out_shape=(shape, shape), in_specs=[SMEM...  2.42 us
  transfers between devices with their start and end apart: 3, of which 3 were waited for; matrix products, arithmetic and copies ran while one was open for 0% of the time, Pallas kernels for 0%

profile of v5, /device:TPU:1, one launch (start us, length us, event | category | flops | bytes accessed | tf_op | source)
XLA Modules:
  0.0 94.7 jit_solution(4824678450819184949)
XLA Ops:
  0.0 1.4 %shard_map.91 = (bf16[16,8,1024]{2,1,0:T(8,128)(2,1)S(1)}, bf16[1024,128]{1,0:T(8,128)(2,1)S(1)}, f32[8,128]{1,0:T(8,128)S(1)}, f32[8,128]{1,0:T(8,128)S(1)}, f3...) custom-call(bf16[8,16384]{1,0:T(8,128)(2,1)} %hidden_hbm.1, f32[1,16384]{1,0:T(1,128)} %bitcast.19, ...), custom_call_target="tpu_custom_call" | custom-call | tf_op jit(solution)/shard_map/pallas_call | solution.py:185
  1.4 23.0 %all_to_all.25 = bf16[16,8,1024]{2,1,0:T(8,128)(2,1)S(1)} all-to-all(bf16[16,8,1024]{2,1,0:T(8,128)(2,1)S(1)} %get-tuple-element.13), channel_id=1, replica_groups={{0,16,34,50,64,80,98,114,128,144,162,178,192,208,226,242},{1,17,35,51,6..., dimensions={0} | all-to-all | bytes 524288 | tf_op jit(solution)/shard_map/all_to_all | solution.py:50
  24.4 0.2 fusion.5
  24.7 0.0 copy-start.1
  24.7 0.4 fusion
  25.1 0.1 fusion.3
  25.2 16.1 %all_to_all.26 = f16[16,8,1152]{2,1,0:T(8,128)(2,1)S(1)} all-to-all(f16[16,8,1152]{2,1,0:T(8,128)(2,1)S(1)} %fusion.3), channel_id=1, replica_groups=mesh['dp'=16,'tensor'=16] {'dp'}, dimensions={0} | all-to-all | bytes 589824 | tf_op jit(solution)/shard_map/all_to_all | solution.py:206
  41.3 0.0 copy-start.3
  41.4 0.0 copy-start.4
  41.4 0.1 shard_map.92.own
  41.5 0.0 copy-start.5
  41.5 2.4 %collective-permute-start = (bf16[8,16,128]{2,1,0:T(8,128)(2,1)S(1)}, bf16[8,16,128]{2,1,0:T(8,128)(2,1)S(1)}, u32[]{:S(2)}, u32[]{:S(2)}) collective-permute-start(bf16[8,16,128]{2,1,0:T(8,128)(2,1)S(1)} %shard_map.92.own), channel_id=1, source_target_pairs={{0,1},{1,0},{2,3},{3,2},{4,5},{5,4},{6,7},{7,6},{8,9},{9,8},{10,11... | collective-permute-start | bytes 98312 | tf_op jit(solution)/shard_map/ppermute | solution.py:60
  43.8 0.9 collective-permute-done.other
  44.7 2.4 %shard_map.93 = (f32[8,8,384]{2,1,0:T(8,128)S(1)}, f32[8,8,384]{2,1,0:T(8,128)S(1)}) custom-call(s32[8]{0:T(128)S(1)} %copy-done.4, s32[8]{0:T(128)S(1)} %copy-done.3, bf16[8,16,128]{2,1,0:T(8,128)(2,1)S(1)} %shard_map.92.own, bf16[8,16,128]{2,1,0:T(8,128)(2,1)S(1)} %collective-permute-done.other, bf16[8,1,2048,128]{3,2,1,0:T(8,128)(2,1)S(1)} %copy-done.2, ...), custom_call_target="tpu_custom_call" | custom-call | tf_op jit(solution)/shard_map/pallas_call | solution.py:219
  47.1 1.2 %collective-permute-start.1 = (f32[8,8,384]{2,1,0:T(8,128)S(1)}, f32[8,8,384]{2,1,0:T(8,128)S(1)}, u32[]{:S(2)}, u32[]{:S(2)}) collective-permute-start(f32[8,8,384]{2,1,0:T(8,128)S(1)} %get-tuple-element.20), channel_id=1, source_target_pairs={{0,1},{1,0},{2,3},{3,2},{4,5},{5,4},{6,7},{7,6},{8,9},{9,8},{10,11... | collective-permute-start | bytes 294920 | tf_op jit(solution)/shard_map/ppermute | solution.py:60
  48.3 0.9 collective-permute-done.1.theirs
  49.3 0.1 shard_map.94
  49.3 15.2 %all_to_all.27 = bf16[16,8,1024]{2,1,0:T(8,128)(2,1)S(1)} all-to-all(bf16[16,8,1024]{2,1,0:T(8,128)(2,1)S(1)} %shard_map.94), channel_id=1, replica_groups=mesh['dp'=16,'tensor'=16] {'dp'}, dimensions={0} | all-to-all | bytes 524288 | tf_op jit(solution)/shard_map/all_to_all | solution.py:237
  64.5 0.5 fusion.2
  65.0 11.7 %all_to_all.28 = bf16[16,8,1024]{2,1,0:T(8,128)(2,1)S(1)} all-to-all(bf16[16,8,1024]{2,1,0:T(8,128)(2,1)S(1)} %fusion.2), channel_id=1, replica_groups={{11,10,1,8,7,6,13,4,3,2,9,0,15,14,5,12},{24,27,26,17,20,23,22,29,16,19,..., dimensions={0} | all-to-all | bytes 524288 | tf_op jit(solution)/shard_map/all_to_all | solution.py:50
  76.7 1.0 %collective-permute-start.2 = (bf16[8,1024]{1,0:T(8,128)(2,1)S(1)}, bf16[8,1024]{1,0:T(8,128)(2,1)S(1)}, u32[]{:S(2)}, u32[]{:S(2)}) collective-permute-start(bf16[8,1024]{1,0:T(8,128)(2,1)S(1)} %reduce_sum.22), channel_id=1, source_target_pairs={{0,178},{1,35},{2,144},{3,129},{4,118},{5,231},{6,84},{7,69},{8,58... | collective-permute-start | bytes 49160 | tf_op jit(solution)/shard_map/ppermute | solution.py:243
  77.7 4.1 %collective-permute-done.2 = bf16[8,1024]{1,0:T(8,128)(2,1)S(1)} collective-permute-done((bf16[8,1024]{1,0:T(8,128)(2,1)S(1)}, bf16[8,1024]{1,0:T(8,128)(2,1)S(1)}, u32[]{:S(2)}, u32[]{:S(2)}) %collective-permute-start.2) | collective-permute-done | bytes 16416 | tf_op jit(solution)/shard_map/ppermute | solution.py:243
  81.8 12.2 %all_to_all.29 = bf16[16,8,1024]{2,1,0:T(8,128)(2,1)S(1)} all-to-all(bf16[16,8,1024]{2,1,0:T(8,128)(2,1)S(1)} %broadcast_in_dim.10), channel_id=1, replica_groups={{9,10,3,8,13,14,7,12,1,2,11,0,5,6,15,4},{24,25,26,19,28,29,30,23,16,17,..., dimensions={0} | all-to-all | bytes 524288 | tf_op jit(solution)/shard_map/all_to_all | solution.py:50
  94.0 0.7 copy.11
  (12 shorter events, 0.1 us)
Async XLA Ops:
  0.0 24.6 %copy-start = (bf16[1024,1024]{1,0:T(8,128)(2,1)S(1)}, bf16[1024,1024]{1,0:T(8,128)(2,1)}, u32[]{:S(2)}) copy-start(bf16[1024,1024]{1,0:T(8,128)(2,1)} %param.11) | copy-start | bytes 6291460
  24.7 16.7 %copy-start.1 = (bf16[8,1,2048,128]{3,2,1,0:T(8,128)(2,1)S(1)}, bf16[8,1,2048,128]{3,2,1,0:T(8,128)(2,1)}, u32[]{:S(2)}) copy-start(bf16[8,1,2048,128]{3,2,1,0:T(8,128)(2,1)} %values.3) | copy-start | bytes 12582916
  41.3 3.4 %copy-start.2 = (bf16[8,1,2048,128]{3,2,1,0:T(8,128)(2,1)S(1)}, bf16[8,1,2048,128]{3,2,1,0:T(8,128)(2,1)}, u32[]{:S(2)}) copy-start(bf16[8,1,2048,128]{3,2,1,0:T(8,128)(2,1)} %keys.1) | copy-start | bytes 12582916
  41.3 3.4 %copy-start.3 = (s32[8]{0:T(128)S(1)}, s32[8]{0:T(128)}, u32[]{:S(2)}) copy-start(s32[8]{0:T(128)} %lengths.1) | copy-start | bytes 100
  41.4 3.4 %copy-start.4 = (s32[8]{0:T(128)S(1)}, s32[8]{0:T(128)}, u32[]{:S(2)}) copy-start(s32[8]{0:T(128)} %parent.1) | copy-start | bytes 100
  41.5 23.0 %copy-start.5 = (bf16[1024,1024]{1,0:T(8,128)(2,1)S(1)}, bf16[1024,1024]{1,0:T(8,128)(2,1)}, u32[]{:S(2)}) copy-start(bf16[1024,1024]{1,0:T(8,128)(2,1)} %param.13) | copy-start | bytes 6291460
  41.5 3.2 %collective-permute-start = (bf16[8,16,128]{2,1,0:T(8,128)(2,1)S(1)}, bf16[8,16,128]{2,1,0:T(8,128)(2,1)S(1)}, u32[]{:S(2)}, u32[]{:S(2)}) collective-permute-start(bf16[8,16,128]{2,1,0:T(8,128)(2,1)S(1)} %shard_map.92.own), channel_id=1, source_target_pairs={{0,1},{1,0},{2,3},{3,2},{4,5},{5,4},{6,7},{7,6},{8,9},{9,8},{10,11... | collective-permute-start | bytes 98312 | tf_op jit(solution)/shard_map/ppermute | solution.py:60
  47.1 2.1 %collective-permute-start.1 = (f32[8,8,384]{2,1,0:T(8,128)S(1)}, f32[8,8,384]{2,1,0:T(8,128)S(1)}, u32[]{:S(2)}, u32[]{:S(2)}) collective-permute-start(f32[8,8,384]{2,1,0:T(8,128)S(1)} %get-tuple-element.20), channel_id=1, source_target_pairs={{0,1},{1,0},{2,3},{3,2},{4,5},{5,4},{6,7},{7,6},{8,9},{9,8},{10,11... | collective-permute-start | bytes 294920 | tf_op jit(solution)/shard_map/ppermute | solution.py:60
  76.7 5.1 %collective-permute-start.2 = (bf16[8,1024]{1,0:T(8,128)(2,1)S(1)}, bf16[8,1024]{1,0:T(8,128)(2,1)S(1)}, u32[]{:S(2)}, u32[]{:S(2)}) collective-permute-start(bf16[8,1024]{1,0:T(8,128)(2,1)S(1)} %reduce_sum.22), channel_id=1, source_target_pairs={{0,178},{1,35},{2,144},{3,129},{4,118},{5,231},{6,84},{7,69},{8,58... | collective-permute-start | bytes 49160 | tf_op jit(solution)/shard_map/ppermute | solution.py:243

commit v6 on v5

--- a/solution.py
+++ b/solution.py
@@ -152,21 +152,29 @@
     for r in range(rows):
         added, top, total = found[r]
         acc = jnp.dot(weights[r], values[parent[r] - base, 0], preferred_element_type=jnp.float32) + added
-        top = jnp.broadcast_to(top, acc.shape)
-        total = jnp.broadcast_to(total, acc.shape)
-        for k, part in enumerate((acc, top, total)):
+        stats = jnp.where(column[:, :hd] < hd // 2, top, total)
+        for k, part in enumerate((acc, stats)):
             keep[:, r, k * hd : (k + 1) * hd] = part[:8]
             send[:, r, k * hd : (k + 1) * hd] = part[8:]
 
 
 def merge_kernel(mine, theirs, out):
-    hd = mine.shape[2] // 3
-    for h in range(mine.shape[0]):
+    heads, rows, width = mine.shape
+    hd = width // 2
+    first = lax.broadcasted_iota(jnp.int32, (rows, hd), 1) < hd // 2
+
+    def spread(stats):
+        turned = pltpu.roll(stats, hd // 2, 1)
+        return jnp.where(first, stats, turned), jnp.where(first, turned, stats)
+
+    for h in range(heads):
         a, b = mine[h], theirs[h]
-        highest = jnp.maximum(a[:, hd : 2 * hd], b[:, hd : 2 * hd])
-        fa = jnp.exp(a[:, hd : 2 * hd] - highest)
-        fb = jnp.exp(b[:, hd : 2 * hd] - highest)
-        total = a[:, 2 * hd :] * fa + b[:, 2 * hd :] * fb
+        top_a, total_a = spread(a[:, hd:])
+        top_b, total_b = spread(b[:, hd:])
+        highest = jnp.maximum(top_a, top_b)
+        fa = jnp.exp(top_a - highest)
+        fb = jnp.exp(top_b - highest)
+        total = total_a * fa + total_b * fb
         head = ((a[:, :hd] * fa + b[:, :hd] * fb) / total).astype(jnp.bfloat16)
         for k in range(out.shape[0]):
             out[k, :, h * hd : (h + 1) * hd] = head
@@ -215,7 +223,7 @@
         compiler_params=pltpu.CompilerParams(vmem_limit_bytes=8 * 2**20),
             )(jnp.sum(parts, axis=0) * (1.0 / SCALE), *tables, value_cache)
     other = core_swap(own)
-    shape = jax.ShapeDtypeStruct((heads, rows, 3 * hd), jnp.float32)
+    shape = jax.ShapeDtypeStruct((heads, rows, 2 * hd), jnp.float32)
     keep, send = pl.pallas_call(
         attention_kernel,
         out_shape=(shape, shape),

time: 95 us -> 95 us (level)
  no operation moved by 1% of the time
where the time goes in v6:
time: 95 us; the launch traced here: 94.7 us
  blocking collectives  78.2 us (82%)
  waiting for transfers between devices  5.82 us (6%)
  starting transfers between devices  4.54 us (5%)
  Pallas kernels  4.04 us (4%)
  matrix products  1.12 us (1%)
    all_to_all x3, blocking collectives, exchange(): lax.all_to_all(value, ('dp', 'tensor'), 0, 0, tiled=True, axis_index_grou...  46.9 us
    all_to_all x1, blocking collectives, per_device(): lax.all_to_all(partial.astype(jnp.float16).reshape(blocks, rows, cols + h...  16.1 us
    all_to_all x1, blocking collectives, per_device(): spread_heads = lax.all_to_all(copies, 'dp', 0, 0, tiled=True)  15.2 us
    ppermute x1, waiting for transfers between devices, per_device(): block = lax.ppermute(block, ('dp', 'tensor'), MOVES)  4.05 us
    ppermute x2, starting transfers between devices, core_swap(): return lax.ppermute(value, 'tensor', [(t, t ^ 1) for t in range(16)])  3.53 us
    pallas_call x1, Pallas kernels, per_device(): pl.pallas_call(attention_kernel, out_shape=(shape, shape), in_specs=[SMEM...  2.4 us
  transfers between devices with their start and end apart: 3, of which 3 were waited for; matrix products, arithmetic and copies ran while one was open for 0% of the time, Pallas kernels for 0%

profile of v6, /device:TPU:1, one launch (start us, length us, event | category | flops | bytes accessed | tf_op | source)
XLA Modules:
  0.0 94.7 jit_solution(5432480793481653168)
XLA Ops:
  0.0 1.4 %shard_map.91 = (bf16[16,8,1024]{2,1,0:T(8,128)(2,1)S(1)}, bf16[1024,128]{1,0:T(8,128)(2,1)S(1)}, f32[8,128]{1,0:T(8,128)S(1)}, f32[8,128]{1,0:T(8,128)S(1)}, f3...) custom-call(bf16[8,16384]{1,0:T(8,128)(2,1)} %hidden_hbm.1, f32[1,16384]{1,0:T(1,128)} %bitcast.19, ...), custom_call_target="tpu_custom_call" | custom-call | tf_op jit(solution)/shard_map/pallas_call | solution.py:193
  1.4 23.0 %all_to_all.25 = bf16[16,8,1024]{2,1,0:T(8,128)(2,1)S(1)} all-to-all(bf16[16,8,1024]{2,1,0:T(8,128)(2,1)S(1)} %get-tuple-element.13), channel_id=1, replica_groups={{0,16,34,50,64,80,98,114,128,144,162,178,192,208,226,242},{1,17,35,51,6..., dimensions={0} | all-to-all | bytes 524288 | tf_op jit(solution)/shard_map/all_to_all | solution.py:50
  24.4 0.2 fusion.5
  24.7 0.0 copy-start.1
  24.7 0.4 fusion
  25.1 0.1 fusion.3
  25.2 16.1 %all_to_all.26 = f16[16,8,1152]{2,1,0:T(8,128)(2,1)S(1)} all-to-all(f16[16,8,1152]{2,1,0:T(8,128)(2,1)S(1)} %fusion.3), channel_id=1, replica_groups=mesh['dp'=16,'tensor'=16] {'dp'}, dimensions={0} | all-to-all | bytes 589824 | tf_op jit(solution)/shard_map/all_to_all | solution.py:214
  41.3 0.0 copy-start.3
  41.4 0.0 copy-start.4
  41.4 0.1 shard_map.92.own
  41.5 0.0 copy-start.5
  41.5 2.4 %collective-permute-start = (bf16[8,16,128]{2,1,0:T(8,128)(2,1)S(1)}, bf16[8,16,128]{2,1,0:T(8,128)(2,1)S(1)}, u32[]{:S(2)}, u32[]{:S(2)}) collective-permute-start(bf16[8,16,128]{2,1,0:T(8,128)(2,1)S(1)} %shard_map.92.own), channel_id=1, source_target_pairs={{0,1},{1,0},{2,3},{3,2},{4,5},{5,4},{6,7},{7,6},{8,9},{9,8},{10,11... | collective-permute-start | bytes 98312 | tf_op jit(solution)/shard_map/ppermute | solution.py:60
  43.8 0.9 collective-permute-done.other
  44.7 2.4 %shard_map.93 = (f32[8,8,256]{2,1,0:T(8,128)S(1)}, f32[8,8,256]{2,1,0:T(8,128)S(1)}) custom-call(s32[8]{0:T(128)S(1)} %copy-done.4, s32[8]{0:T(128)S(1)} %copy-done.3, bf16[8,16,128]{2,1,0:T(8,128)(2,1)S(1)} %shard_map.92.own, bf16[8,16,128]{2,1,0:T(8,128)(2,1)S(1)} %collective-permute-done.other, bf16[8,1,2048,128]{3,2,1,0:T(8,128)(2,1)S(1)} %copy-done.2, ...), custom_call_target="tpu_custom_call" | custom-call | tf_op jit(solution)/shard_map/pallas_call | solution.py:227
  47.1 1.2 %collective-permute-start.1 = (f32[8,8,256]{2,1,0:T(8,128)S(1)}, f32[8,8,256]{2,1,0:T(8,128)S(1)}, u32[]{:S(2)}, u32[]{:S(2)}) collective-permute-start(f32[8,8,256]{2,1,0:T(8,128)S(1)} %get-tuple-element.20), channel_id=1, source_target_pairs={{0,1},{1,0},{2,3},{3,2},{4,5},{5,4},{6,7},{7,6},{8,9},{9,8},{10,11... | collective-permute-start | bytes 196616 | tf_op jit(solution)/shard_map/ppermute | solution.py:60
  48.3 0.9 collective-permute-done.1.theirs
  49.2 0.1 shard_map.94
  49.3 15.2 %all_to_all.27 = bf16[16,8,1024]{2,1,0:T(8,128)(2,1)S(1)} all-to-all(bf16[16,8,1024]{2,1,0:T(8,128)(2,1)S(1)} %shard_map.94), channel_id=1, replica_groups=mesh['dp'=16,'tensor'=16] {'dp'}, dimensions={0} | all-to-all | bytes 524288 | tf_op jit(solution)/shard_map/all_to_all | solution.py:245
  64.5 0.5 fusion.2
  65.0 11.7 %all_to_all.28 = bf16[16,8,1024]{2,1,0:T(8,128)(2,1)S(1)} all-to-all(bf16[16,8,1024]{2,1,0:T(8,128)(2,1)S(1)} %fusion.2), channel_id=1, replica_groups={{11,10,1,8,7,6,13,4,3,2,9,0,15,14,5,12},{24,27,26,17,20,23,22,29,16,19,..., dimensions={0} | all-to-all | bytes 524288 | tf_op jit(solution)/shard_map/all_to_all | solution.py:50
  76.7 1.0 %collective-permute-start.2 = (bf16[8,1024]{1,0:T(8,128)(2,1)S(1)}, bf16[8,1024]{1,0:T(8,128)(2,1)S(1)}, u32[]{:S(2)}, u32[]{:S(2)}) collective-permute-start(bf16[8,1024]{1,0:T(8,128)(2,1)S(1)} %reduce_sum.22), channel_id=1, source_target_pairs={{0,178},{1,35},{2,144},{3,129},{4,118},{5,231},{6,84},{7,69},{8,58... | collective-permute-start | bytes 49160 | tf_op jit(solution)/shard_map/ppermute | solution.py:251
  77.7 4.1 %collective-permute-done.2 = bf16[8,1024]{1,0:T(8,128)(2,1)S(1)} collective-permute-done((bf16[8,1024]{1,0:T(8,128)(2,1)S(1)}, bf16[8,1024]{1,0:T(8,128)(2,1)S(1)}, u32[]{:S(2)}, u32[]{:S(2)}) %collective-permute-start.2) | collective-permute-done | bytes 16416 | tf_op jit(solution)/shard_map/ppermute | solution.py:251
  81.8 12.2 %all_to_all.29 = bf16[16,8,1024]{2,1,0:T(8,128)(2,1)S(1)} all-to-all(bf16[16,8,1024]{2,1,0:T(8,128)(2,1)S(1)} %broadcast_in_dim.10), channel_id=1, replica_groups={{9,10,3,8,13,14,7,12,1,2,11,0,5,6,15,4},{24,25,26,19,28,29,30,23,16,17,..., dimensions={0} | all-to-all | bytes 524288 | tf_op jit(solution)/shard_map/all_to_all | solution.py:50
  94.0 0.7 copy.11
  (12 shorter events, 0.1 us)
Async XLA Ops:
  0.0 24.6 %copy-start = (bf16[1024,1024]{1,0:T(8,128)(2,1)S(1)}, bf16[1024,1024]{1,0:T(8,128)(2,1)}, u32[]{:S(2)}) copy-start(bf16[1024,1024]{1,0:T(8,128)(2,1)} %param.11) | copy-start | bytes 6291460
  24.7 16.7 %copy-start.1 = (bf16[8,1,2048,128]{3,2,1,0:T(8,128)(2,1)S(1)}, bf16[8,1,2048,128]{3,2,1,0:T(8,128)(2,1)}, u32[]{:S(2)}) copy-start(bf16[8,1,2048,128]{3,2,1,0:T(8,128)(2,1)} %values.3) | copy-start | bytes 12582916
  41.3 3.4 %copy-start.2 = (bf16[8,1,2048,128]{3,2,1,0:T(8,128)(2,1)S(1)}, bf16[8,1,2048,128]{3,2,1,0:T(8,128)(2,1)}, u32[]{:S(2)}) copy-start(bf16[8,1,2048,128]{3,2,1,0:T(8,128)(2,1)} %keys.1) | copy-start | bytes 12582916
  41.3 3.4 %copy-start.3 = (s32[8]{0:T(128)S(1)}, s32[8]{0:T(128)}, u32[]{:S(2)}) copy-start(s32[8]{0:T(128)} %lengths.1) | copy-start | bytes 100
  41.4 3.4 %copy-start.4 = (s32[8]{0:T(128)S(1)}, s32[8]{0:T(128)}, u32[]{:S(2)}) copy-start(s32[8]{0:T(128)} %parent.1) | copy-start | bytes 100
  41.5 23.0 %copy-start.5 = (bf16[1024,1024]{1,0:T(8,128)(2,1)S(1)}, bf16[1024,1024]{1,0:T(8,128)(2,1)}, u32[]{:S(2)}) copy-start(bf16[1024,1024]{1,0:T(8,128)(2,1)} %param.13) | copy-start | bytes 6291460
  41.5 3.2 %collective-permute-start = (bf16[8,16,128]{2,1,0:T(8,128)(2,1)S(1)}, bf16[8,16,128]{2,1,0:T(8,128)(2,1)S(1)}, u32[]{:S(2)}, u32[]{:S(2)}) collective-permute-start(bf16[8,16,128]{2,1,0:T(8,128)(2,1)S(1)} %shard_map.92.own), channel_id=1, source_target_pairs={{0,1},{1,0},{2,3},{3,2},{4,5},{5,4},{6,7},{7,6},{8,9},{9,8},{10,11... | collective-permute-start | bytes 98312 | tf_op jit(solution)/shard_map/ppermute | solution.py:60
  47.1 2.1 %collective-permute-start.1 = (f32[8,8,256]{2,1,0:T(8,128)S(1)}, f32[8,8,256]{2,1,0:T(8,128)S(1)}, u32[]{:S(2)}, u32[]{:S(2)}) collective-permute-start(f32[8,8,256]{2,1,0:T(8,128)S(1)} %get-tuple-element.20), channel_id=1, source_target_pairs={{0,1},{1,0},{2,3},{3,2},{4,5},{5,4},{6,7},{7,6},{8,9},{9,8},{10,11... | collective-permute-start | bytes 196616 | tf_op jit(solution)/shard_map/ppermute | solution.py:60
  76.7 5.1 %collective-permute-start.2 = (bf16[8,1024]{1,0:T(8,128)(2,1)S(1)}, bf16[8,1024]{1,0:T(8,128)(2,1)S(1)}, u32[]{:S(2)}, u32[]{:S(2)}) collective-permute-start(bf16[8,1024]{1,0:T(8,128)(2,1)S(1)} %reduce_sum.22), channel_id=1, source_target_pairs={{0,178},{1,35},{2,144},{3,129},{4,118},{5,231},{6,84},{7,69},{8,58... | collective-permute-start | bytes 49160 | tf_op jit(solution)/shard_map/ppermute | solution.py:251
